TPU v7x, 128 devices: a whole 4x4x4 slice. The times are simulated.
128 devices in a mesh: dp: 32 (over y, x, core), pipe: 4 (over z).
Axes of the slice: x: 4, y: 4, z: 4, core: 2. Of those that a mesh axis runs over, the one named last changes fastest.
Arguments:
- latents: bfloat16 [96, 192, 320], P('dp'), may hold values from -6 to 6
- cotangent: bfloat16 [96, 192, 320], P('dp'), may hold values from -0.109375 to 0.109375
- timesteps: int32 [96], P('dp'), may hold values from 0 to 999
- layer_count: int32 [4], P('pipe'), may hold values from 1 to 3, as said below
- up_weight: bfloat16 [4, 3, 320, 1280], P('pipe'), may hold values from -0.3125 to 0.3125
- down_weight: bfloat16 [4, 3, 1280, 320], P('pipe'), may hold values from -0.15625 to 0.15625
- time_weight: bfloat16 [4, 3, 320, 640], P('pipe'), may hold values from -0.3125 to 0.3125
- skip_weight: bfloat16 [4, 320, 320], P('pipe'), may hold values from -0.3125 to 0.3125
Outputs:
- grad_up: float32 [4, 3, 320, 1280], P('pipe', None, 'dp')
- grad_down: float32 [4, 3, 1280, 320], P('pipe', None, 'dp')
- grad_time: float32 [4, 3, 320, 640], P('pipe', None, 'dp')
- grad_skip: float32 [4, 320, 320], P('pipe', 'dp')
Inputs may be any that keep to these rules, and one draw needn't show every extreme that they name: `layer_count`: some section runs all 3 layer slots and some section runs only one.
All inputs are finite; a program needn't handle non-finite values.
Results may differ from a plain program's by a relative error of at most 0.033.
Values may be sent and summed in bfloat16 or wider, within the bound.
No kernel may reach another device: no remote copies, remote signals or barrier semaphores. Data moves between devices by JAX's collectives and lax.ppermute only.
A program may use at most 192 MiB of HBM per device.

v0:
```python
import functools
import math

import jax
import jax.numpy as jnp
import ml_dtypes
import numpy as np
from jax import lax
from jax.experimental import pallas as pl
from jax.experimental.pallas import tpu as pltpu
from jax.sharding import Mesh
from jax.sharding import PartitionSpec as P

EPSILON = 1e-06
BF16 = jnp.bfloat16
F32 = jnp.float32
CHUNK = 256
SECTION_VMEM = 53 * 1024 * 1024
GRAD_VMEM = 56 * 1024 * 1024
ANY = pl.BlockSpec(memory_space=pl.ANY)
SMEM = pl.BlockSpec(memory_space=pltpu.SMEM)
NT = (((1,), (1,)), ((), ()))
TN = (((0,), (0,)), ((), ()))


def embedding(timesteps, halfway):
    frequency = jnp.exp(-math.log(10000.0) * jnp.arange(halfway, dtype=F32) / halfway)
    angles = timesteps.astype(F32)[..., None] * frequency
    return jnp.concatenate([jnp.sin(angles), jnp.cos(angles)], axis=-1)


def nt_dot(left, right):
    return lax.dot_general(left, right, NT, preferred_element_type=F32)


def sigmoid(value):
    return 0.5 * jnp.tanh(0.5 * value) + 0.5


def forward_kernel(tick, has_saved, has_skip, samples, slots, sections, width, *refs):
    refs = list(refs)
    scal, mod, latents, incoming, up, down, skip_weight = refs[:7]
    del refs[:7]
    skip_in = refs.pop(0) if has_skip else None
    if has_saved:
        del refs[:3]
    out, states, pres, skips = refs[:4]
    xv, sv, modv, upv, downv, skwv, statev, prev, acc, hidv, sems = refs[4:]
    stage, count = scal[0], scal[1]
    sample = tick - 2 * stage
    hidden_width = upv.shape[2]
    half = sections // 2

    @pl.when((sample >= 0) & (sample < samples))
    def _():
        copy_latents = pltpu.make_async_copy(latents.at[sample], xv, sems.at[0])
        copy_incoming = pltpu.make_async_copy(incoming, xv, sems.at[0])
        copy_mod = pltpu.make_async_copy(mod.at[sample], modv, sems.at[1])
        copy_skw = pltpu.make_async_copy(skip_weight, skwv, sems.at[2])

        def copy_up(j):
            return pltpu.make_async_copy(up.at[j], upv.at[j], sems.at[4 + j])

        def copy_down(j):
            return pltpu.make_async_copy(down.at[j], downv.at[j], sems.at[4 + slots + j])

        def save_state(j):
            return pltpu.make_async_copy(
                statev.at[j], states.at[sample, j], sems.at[4 + 2 * slots + j]
            )

        def save_pre(j):
            return pltpu.make_async_copy(prev.at[j], pres.at[sample, j], sems.at[4 + 3 * slots + j])

        save_skip = pltpu.make_async_copy(sv, skips.at[sample], sems.at[3])

        @pl.when(stage == 0)
        def _():
            copy_latents.start()

        @pl.when(stage != 0)
        def _():
            copy_incoming.start()

        copy_mod.start()
        decoder = stage >= half

        @pl.when(decoder)
        def _():
            copy_skw.start()

        @pl.loop(0, count)
        def _(j):
            copy_up(j).start()
            copy_down(j).start()

        copy_incoming.wait()
        acc[...] = xv[...].astype(F32)

        @pl.when(decoder)
        def _():
            if has_skip:
                copy_skip = pltpu.make_async_copy(skip_in, sv, sems.at[3])

                @pl.when(stage == sections - 1)
                def _():
                    copy_skip.start()
                    copy_skip.wait()

                @pl.when(stage != sections - 1)
                def _():
                    sv[...] = xv[...]

            else:
                sv[...] = xv[...]
            save_skip.start()
            copy_skw.wait()
            acc[...] += jnp.dot(sv[...], skwv[...], preferred_element_type=F32)

        copy_mod.wait()

        @pl.loop(0, count)
        def _(j):
            copy_up(j).wait()
            copy_down(j).wait()
            state = acc[...]
            statev[j] = state
            scaling = modv[pl.ds(j, 1), :width]
            offset = modv[pl.ds(j, 1), width:]
            inverse = lax.rsqrt(jnp.mean(state * state, axis=-1, keepdims=True) + EPSILON)
            normed = (state * inverse * (1.0 + scaling) + offset).astype(BF16)
            for start in range(0, hidden_width, CHUNK):
                cols = slice(start, start + CHUNK)
                pre = jnp.dot(normed, upv[j, :, cols], preferred_element_type=F32)
                prev[j, :, cols] = pre.astype(BF16)
                hidv[:, cols] = (pre * sigmoid(pre)).astype(BF16)
            acc[...] = state + nt_dot(hidv[...], downv[j])
            save_state(j).start()
            save_pre(j).start()

        xv[...] = acc[...].astype(BF16)
        save_out = pltpu.make_async_copy(xv, out, sems.at[0])
        save_out.start()

        @pl.loop(0, count)
        def _(j):
            save_state(j).wait()
            save_pre(j).wait()

        @pl.when(decoder)
        def _():
            save_skip.wait()

        save_out.wait()


def forward_call(tick, scal, mod, latents, incoming, up, down, skip_weight, skip_in, saved):
    samples, rows, width = latents.shape
    slots, _, hidden_width = up.shape
    shapes = (
        jax.ShapeDtypeStruct((rows, width), BF16),
        jax.ShapeDtypeStruct((samples, slots, rows, width), F32),
        jax.ShapeDtypeStruct((samples, slots, rows, hidden_width), BF16),
        jax.ShapeDtypeStruct((samples, rows, width), BF16),
    )
    operands = [scal, mod, latents, incoming, up, down, skip_weight]
    if skip_in is not None:
        operands.append(skip_in)
    aliases = {}
    if saved is not None:
        aliases = {len(operands) + i: 1 + i for i in range(3)}
        operands += list(saved)
    out = pl.pallas_call(
        functools.partial(
            forward_kernel,
            tick,
            saved is not None,
            skip_in is not None,
            samples,
            slots,
            4,
            width,
        ),
        out_shape=shapes,
        in_specs=[SMEM] + [ANY] * (len(operands) - 1),
        out_specs=(ANY,) * 4,
        input_output_aliases=aliases,
        scratch_shapes=[
            pltpu.VMEM((rows, width), BF16),
            pltpu.VMEM((rows, width), BF16),
            pltpu.VMEM((slots, 2 * width), F32),
            pltpu.VMEM((slots, width, hidden_width), BF16),
            pltpu.VMEM((slots, width, hidden_width), BF16),
            pltpu.VMEM((width, width), BF16),
            pltpu.VMEM((slots, rows, width), F32),
            pltpu.VMEM((slots, rows, hidden_width), BF16),
            pltpu.VMEM((rows, width), F32),
            pltpu.VMEM((rows, hidden_width), BF16),
            pltpu.SemaphoreType.DMA((4 + 4 * slots,)),
        ],
        compiler_params=pltpu.CompilerParams(vmem_limit_bytes=SECTION_VMEM),
        cost_estimate=pl.CostEstimate(
            flops=slots * rows * width * hidden_width * 4,
            bytes_accessed=8_000_000,
            transcendentals=0,
        ),
        name=f"section_forward_{tick}",
    )(*operands)
    return out[0], out[1:]


def backward_kernel(tick, has_saved, has_skip, samples, slots, sections, width, *refs):
    refs = list(refs)
    scal, mod, cotangent, incoming, up, down, skip_weight, states, pres = refs[:9]
    del refs[:9]
    skip_grad = refs.pop(0) if has_skip else None
    if has_saved:
        del refs[:6]
    out, out_skip, norms, outs, hiddens, dpres, mod_grads, firsts = refs[:8]
    gv, hv, modv, upv, downv, skwv, statev, prev, acc, nv, ov, hidv, dpv, mgv, fv, sems = refs[8:]
    stage, count = scal[0], scal[1]
    sample = tick - 2 * (sections - 1 - stage)
    hidden_width = upv.shape[2]
    half = sections // 2

    @pl.when((sample >= 0) & (sample < samples))
    def _():
        copy_cot = pltpu.make_async_copy(cotangent.at[sample], gv, sems.at[0])
        copy_incoming = pltpu.make_async_copy(incoming, gv, sems.at[0])
        copy_mod = pltpu.make_async_copy(mod.at[sample], modv, sems.at[1])
        copy_skw = pltpu.make_async_copy(skip_weight, skwv, sems.at[2])


        def copy(group, j, source, target):
            return pltpu.make_async_copy(source, target, sems.at[4 + group * slots + j])

        def loads(j):
            return (
                copy(0, j, down.at[j], downv.at[j]),
                copy(1, j, pres.at[sample, j], prev.at[j]),
                copy(2, j, up.at[j], upv.at[j]),
                copy(3, j, states.at[sample, j], statev.at[j]),
            )

        def saves(j):
            return (
                copy(4, j, nv.at[j], norms.at[j, sample]),
                copy(5, j, ov.at[j], outs.at[j, sample]),
                copy(6, j, hidv.at[j], hiddens.at[j, sample]),
                copy(7, j, dpv.at[j], dpres.at[j, sample]),
            )

        @pl.when(stage == sections - 1)
        def _():
            copy_cot.start()

        @pl.when(stage != sections - 1)
        def _():
            copy_incoming.start()

        if has_skip:
            copy_skip = pltpu.make_async_copy(skip_grad, hv, sems.at[3])

            @pl.when(stage == 0)
            def _():
                copy_skip.start()

        copy_mod.start()
        decoder = stage >= half

        @pl.loop(0, count)
        def _(i):
            for load in loads(count - 1 - i):
                load.start()

        @pl.when(decoder)
        def _():
            copy_skw.start()

        copy_incoming.wait()
        if has_skip:

            @pl.when(stage == 0)
            def _():
                copy_skip.wait()
                acc[...] = (gv[...] + hv[...]).astype(F32)

            @pl.when(stage != 0)
            def _():
                acc[...] = gv[...].astype(F32)

        else:
            acc[...] = gv[...].astype(F32)
        copy_mod.wait()
        mgv[...] = jnp.zeros_like(mgv)

        @pl.loop(0, count)
        def _(i):
            j = count - 1 - i
            for load in loads(j):
                load.wait()
            grad = acc[...]
            grad_b = grad.astype(BF16)
            ov[j] = grad_b
            for start in range(0, hidden_width, CHUNK):
                cols = slice(start, start + CHUNK)
                grad_hidden = jnp.dot(grad_b, downv[j, :, cols], preferred_element_type=F32)
                pre = prev[j, :, cols].astype(F32)
                gate = sigmoid(pre)
                hidden = pre * gate
                hidv[j, :, cols] = hidden.astype(BF16)
                dpv[j, :, cols] = (grad_hidden * (gate + hidden * (1.0 - gate))).astype(BF16)
            total = nt_dot(dpv[j], upv[j])
            state = statev[j]
            scaling = 1.0 + modv[pl.ds(j, 1), :width]
            offset = modv[pl.ds(j, 1), width:]
            inverse = lax.rsqrt(jnp.mean(state * state, axis=-1, keepdims=True) + EPSILON)
            unit = state * inverse
            nv[j] = (unit * scaling + offset).astype(BF16)
            grad_norm = total.astype(BF16).astype(F32)
            scaled = grad_norm * unit
            mgv[pl.ds(j, 1), :width] = jnp.sum(scaled, axis=0, keepdims=True)
            mgv[pl.ds(j, 1), width:] = jnp.sum(grad_norm, axis=0, keepdims=True)
            inner = jnp.mean(scaled * scaling, axis=-1, keepdims=True)
            acc[...] = grad + inverse * (grad_norm * scaling - unit * inner)
            for save in saves(j):
                save.start()

        save_mods = pltpu.make_async_copy(mgv, mod_grads.at[sample], sems.at[1])
        save_mods.start()
        first = acc[...].astype(BF16)
        fv[...] = first
        gv[...] = first
        save_first = pltpu.make_async_copy(fv, firsts.at[sample], sems.at[3])
        save_first.start()

        @pl.when(decoder)
        def _():
            copy_skw.wait()
            grad_skip = nt_dot(first, skwv[...]).astype(BF16)
            hv[...] = grad_skip

            @pl.when(stage == half)
            def _():
                gv[...] = first + grad_skip

        save_down = pltpu.make_async_copy(gv, out, sems.at[0])
        save_skip = pltpu.make_async_copy(hv, out_skip, sems.at[2])
        save_down.start()

        @pl.when(stage == sections - 1)
        def _():
            save_skip.start()
            save_skip.wait()

        @pl.loop(0, count)
        def _(j):
            for save in saves(j):
                save.wait()

        save_first.wait()
        save_mods.wait()
        save_down.wait()


def backward_call(
    tick, scal, mod, cotangent, incoming, up, down, skip_weight, states, pres, skip_grad, saved
):
    samples, rows, width = cotangent.shape
    slots, _, hidden_width = up.shape
    narrow = (rows, width)
    wide = (rows, hidden_width)
    shapes = (
        jax.ShapeDtypeStruct(narrow, BF16),
        jax.ShapeDtypeStruct(narrow, BF16),
        jax.ShapeDtypeStruct((slots, samples, *narrow), BF16),
        jax.ShapeDtypeStruct((slots, samples, *narrow), BF16),
        jax.ShapeDtypeStruct((slots, samples, *wide), BF16),
        jax.ShapeDtypeStruct((slots, samples, *wide), BF16),
        jax.ShapeDtypeStruct((samples, slots, 2 * width), F32),
        jax.ShapeDtypeStruct((samples, *narrow), BF16),
    )
    operands = [scal, mod, cotangent, incoming, up, down, skip_weight, states, pres]
    if skip_grad is not None:
        operands.append(skip_grad)
    aliases = {}
    if saved is not None:
        aliases = {len(operands) + i: 2 + i for i in range(6)}
        operands += list(saved)
    out = pl.pallas_call(
        functools.partial(
            backward_kernel,
            tick,
            saved is not None,
            skip_grad is not None,
            samples,
            slots,
            4,
            width,
        ),
        out_shape=shapes,
        in_specs=[SMEM] + [ANY] * (len(operands) - 1),
        out_specs=(ANY,) * len(shapes),
        input_output_aliases=aliases,
        scratch_shapes=[
            pltpu.VMEM(narrow, BF16),
            pltpu.VMEM(narrow, BF16),
            pltpu.VMEM((slots, 2 * width), F32),
            pltpu.VMEM((slots, width, hidden_width), BF16),
            pltpu.VMEM((slots, width, hidden_width), BF16),
            pltpu.VMEM((width, width), BF16),
            pltpu.VMEM((slots, *narrow), F32),
            pltpu.VMEM((slots, *wide), BF16),
            pltpu.VMEM(narrow, F32),
            pltpu.VMEM((slots, *narrow), BF16),
            pltpu.VMEM((slots, *narrow), BF16),
            pltpu.VMEM((slots, *wide), BF16),
            pltpu.VMEM((slots, *wide), BF16),
            pltpu.VMEM((slots, 2 * width), F32),
            pltpu.VMEM(narrow, BF16),
            pltpu.SemaphoreType.DMA((4 + 8 * slots,)),
        ],
        compiler_params=pltpu.CompilerParams(vmem_limit_bytes=SECTION_VMEM),
        cost_estimate=pl.CostEstimate(
            flops=slots * rows * width * hidden_width * 4,
            bytes_accessed=14_000_000,
            transcendentals=0,
        ),
        name=f"section_backward_{tick}",
    )(*operands)
    return out[0], out[1], out[2:]


def up_grad_kernel(scal, norm, dpre, order, condition, mod_grads, mine, theirs, product):
    count, core = scal[1], scal[2]
    slot = pl.program_id(0)
    slots = pl.num_programs(0) - 1
    block, lanes = mine.shape[2:]

    @pl.when(slot < count)
    def _():
        placed = jnp.dot(norm[0], order[...], preferred_element_type=F32).astype(BF16)
        for start in range(0, dpre.shape[2], CHUNK):
            cols = slice(start, start + CHUNK)
            product[:, cols] = lax.dot_general(
                placed, dpre[0, :, cols], TN, preferred_element_type=F32
            )

    @pl.when((slot >= count) & (slot < slots))
    def _():
        product[...] = jnp.zeros_like(product)

    @pl.when(slot == slots)
    def _():
        for half in range(2):
            product[:, half * lanes : (half + 1) * lanes] = time_product(condition, mod_grads, half)

    for i in range(4):
        for half in range(2):
            cols = slice(half * lanes, (half + 1) * lanes)
            low = pl.multiple_of((core * 4 + i) * block, 8)
            mine[i, half] = product[pl.ds(low, block), cols].astype(BF16)
            low = pl.multiple_of(((1 - core) * 4 + i) * block, 8)
            theirs[i, half] = product[pl.ds(low, block), cols].astype(BF16)


def time_product(condition, mod_grads, slot):
    total = condition[:, 0:1] * mod_grads[0, slot : slot + 1, :]
    for sample in range(1, mod_grads.shape[0]):
        total = total + (
            condition[:, sample : sample + 1] * mod_grads[sample, slot : slot + 1, :]
        )
    return total


def whole(shape):
    return pl.BlockSpec(shape, lambda j: (0,) * len(shape))


def up_grad_call(scal, norms, dpres, order, condition, mod_grads):
    slots, rows, width = norms.shape
    hidden_width = dpres.shape[2]
    block = width // 8
    last = slots - 1
    shape = jax.ShapeDtypeStruct((4, 2 * slots + 2, block, hidden_width // 2), BF16)
    spec = pl.BlockSpec((4, 2, block, hidden_width // 2), lambda j: (0, j, 0, 0))
    return pl.pallas_call(
        up_grad_kernel,
        grid=(slots + 1,),
        out_shape=(shape, shape),
        in_specs=[
            SMEM,
            pl.BlockSpec((1, rows, width), lambda j: (jnp.minimum(j, last), 0, 0)),
            pl.BlockSpec((1, rows, hidden_width), lambda j: (jnp.minimum(j, last), 0, 0)),
            whole((width, width)),
            whole(condition.shape),
            whole(mod_grads.shape),
        ],
        out_specs=(spec, spec),
        scratch_shapes=[pltpu.VMEM((width, hidden_width), F32)],
        compiler_params=pltpu.CompilerParams(vmem_limit_bytes=GRAD_VMEM),
        cost_estimate=pl.CostEstimate(
            flops=2 * slots * rows * width * hidden_width,
            bytes_accessed=12_000_000,
            transcendentals=0,
        ),
        name="up_grad",
    )(scal, norms, dpres, order, condition, mod_grads)


def down_grad_kernel(
    scal,
    hidden,
    out_grad,
    skip_in,
    first,
    order,
    condition,
    mod_grads,
    mine,
    theirs,
    product,
    prod_time,
    prod_skip,
):
    stage, count, core = scal[0], scal[1], scal[2]
    slot = pl.program_id(0)
    slots = pl.num_programs(0) - 1
    block, lanes = mine.shape[2:]
    width = lanes // 2

    @pl.when(slot < count)
    def _():
        for start in range(0, hidden.shape[2], CHUNK):
            cols = slice(start, start + CHUNK)
            product[cols, :] = lax.dot_general(
                hidden[0, :, cols], out_grad[0], TN, preferred_element_type=F32
            )

    @pl.when((slot >= count) & (slot < slots))
    def _():
        product[...] = jnp.zeros_like(product)

    @pl.when(slot == slots)
    def _():
        prod_skip[...] = jnp.zeros_like(prod_skip)
        prod_time[...] = time_product(condition, mod_grads, 2)

    @pl.when((slot == slots) & (stage >= 2))
    def _():
        placed = jnp.dot(skip_in[...], order[...], preferred_element_type=F32).astype(BF16)
        prod_skip[:, :width] = lax.dot_general(placed, first[...], TN, preferred_element_type=F32)

    @pl.when(slot < slots)
    def _():
        for target, side in ((mine, core), (theirs, 1 - core)):
            for y in range(4):
                for pair in range(2):
                    low = pl.multiple_of((8 * y + 4 * pair + side) * block, 8)
                    high = pl.multiple_of((8 * y + 4 * pair + 2 + side) * block, 8)
                    target[y, pair] = jnp.concatenate(
                        [product[pl.ds(low, block), :], product[pl.ds(high, block), :]], axis=1
                    ).astype(BF16)

    @pl.when(slot == slots)
    def _():
        for target, side in ((mine, core), (theirs, 1 - core)):
            for y in range(4):
                low = pl.multiple_of((side * 4 + y) * block, 8)
                target[y, 0] = prod_time[pl.ds(low, block), :].astype(BF16)
                target[y, 1] = prod_skip[pl.ds(low, block), :].astype(BF16)


def down_grad_call(scal, hiddens, outs, skips, firsts, order, condition, mod_grads):
    slots, rows, hidden_width = hiddens.shape
    width = outs.shape[2]
    block = width // 8
    shape = jax.ShapeDtypeStruct((4, 2 * slots + 2, block, 2 * width), BF16)
    spec = pl.BlockSpec((4, 2, block, 2 * width), lambda j: (0, j, 0, 0))
    last = slots - 1
    return pl.pallas_call(
        down_grad_kernel,
        grid=(slots + 1,),
        out_shape=(shape, shape),
        in_specs=[
            SMEM,
            pl.BlockSpec((1, rows, hidden_width), lambda j: (jnp.minimum(j, last), 0, 0)),
            pl.BlockSpec((1, rows, width), lambda j: (jnp.minimum(j, last), 0, 0)),
            whole((rows, width)),
            whole((rows, width)),
            whole((width, width)),
            whole(condition.shape),
            whole(mod_grads.shape),
        ],
        out_specs=(spec, spec),
        scratch_shapes=[
            pltpu.VMEM((hidden_width, width), F32),
            pltpu.VMEM((width, 2 * width), F32),
            pltpu.VMEM((width, 2 * width), F32),
        ],
        compiler_params=pltpu.CompilerParams(vmem_limit_bytes=GRAD_VMEM),
        cost_estimate=pl.CostEstimate(
            flops=2 * slots * rows * width * hidden_width,
            bytes_accessed=12_000_000,
            transcendentals=0,
        ),
        name="down_grad",
    )(scal, hiddens, outs, skips, firsts, order, condition, mod_grads)


def block_order(width, first, second):
    block = width // 32
    matrix = np.zeros((width, width), ml_dtypes.bfloat16)
    for y in range(4):
        for x in range(4):
            for core in range(2):
                where = {"x": x, "y": y}
                place = (core * 4 + where[first]) * 4 + where[second]
                source = 8 * y + 2 * x + core
                for r in range(block):
                    matrix[source * block + r, place * block + r] = 1
    return jnp.asarray(matrix)


def shifted(size, distance):
    return [(i, (i + distance) % size) for i in range(size)]


def scattered(pieces, axis, out_type):
    size = lax.axis_size(axis)
    index = lax.axis_index(axis)
    arrived = [
        lax.ppermute(pieces(lax.rem(index + d, size)), axis, shifted(size, d)) for d in (2, 1, 3)
    ]
    total = pieces(index).astype(F32)
    for value in arrived:
        total = total + value.astype(F32)
    return total.astype(out_type)


def halved(pieces, axis):
    size = lax.axis_size(axis)
    index = lax.axis_index(axis)
    own, ahead, across, behind = (pieces(lax.rem(index + d, size)) for d in (0, 1, 2, 3))
    cut = own.shape[0] // 2
    forward, backward = shifted(size, 1), shifted(size, size - 1)
    from_behind = lax.ppermute(jnp.concatenate([across[:cut], ahead[cut:]]), axis, forward)
    from_ahead = lax.ppermute(jnp.concatenate([across[cut:], behind[:cut]]), axis, backward)
    rest = own.shape[0] - cut
    passed_on = lax.ppermute(add(ahead[:cut], from_behind[:cut]), axis, forward)
    passed_back = lax.ppermute(add(behind[cut:], from_ahead[:rest]), axis, backward)
    low = add(own[:cut], from_ahead[rest:], passed_on)
    high = add(own[cut:], from_behind[cut:], passed_back)
    return jnp.concatenate([low, high])


def add(*terms):
    total = terms[0].astype(F32)
    for term in terms[1:]:
        total = total + term.astype(F32)
    return total.astype(BF16)


def take(value, index, dim):
    return lax.dynamic_index_in_dim(value, index, dim, keepdims=False)


def per_device(
    latents, cotangent, timesteps, layer_count, up_weight, down_weight, time_weight, skip_weight
):
    sections = lax.axis_size("pipe")
    stage = lax.axis_index("pipe")
    core = lax.axis_index("core")
    samples, rows, width = latents.shape
    up, down, skip_mat = up_weight[0], down_weight[0].swapaxes(1, 2), skip_weight[0]
    slots, _, hidden_width = up.shape
    scal = jnp.stack([stage, layer_count[0], core, core]).astype(jnp.int32)
    condition = jax.nn.silu(embedding(timesteps, width // 2)).astype(BF16)
    modulation = jnp.einsum("mt,jtc->mjc", condition, time_weight[0], preferred_element_type=F32)
    order_x = block_order(width, "x", "y")
    order_y = block_order(width, "y", "x")

    def columns(order):
        placed = lax.dot_general(order, condition, (((0,), (1,)), ((), ())))
        return placed.astype(F32)

    condition_x, condition_y = columns(order_x), columns(order_y)

    ticks = samples + 2 * (sections - 1)
    empty = jnp.zeros((rows, width), BF16)
    moved = {}
    skips_moved = {}
    saved = None
    for tick in range(ticks):
        incoming = moved.get(tick - 2, empty)
        sent, saved = forward_call(
            tick,
            scal,
            modulation,
            latents,
            incoming,
            up,
            down,
            skip_mat,
            skips_moved.get(tick - 2 * (sections - 1)),
            saved,
        )
        pairs = [(z, z + 1) for z in range(sections - 1) if 0 <= tick - 2 * z < samples]
        if pairs:
            moved[tick] = lax.ppermute(sent, "pipe", pairs)
        if tick < samples:
            skips_moved[tick] = lax.ppermute(sent, "pipe", [(0, sections - 1)])
    states, pres, skips = saved

    moved = {}
    skips_moved = {}
    kept = None
    for tick in range(ticks):
        incoming = moved.get(tick - 2, empty)
        sent, sent_skip, kept = backward_call(
            tick,
            scal,
            modulation,
            cotangent,
            incoming,
            up,
            down,
            skip_mat,
            states,
            pres,
            skips_moved.get(tick - 2 * (sections - 1)),
            kept,
        )
        pairs = [
            (z, z - 1)
            for z in range(1, sections)
            if 0 <= tick - 2 * (sections - 1 - z) < samples
        ]
        if pairs:
            moved[tick] = lax.ppermute(sent, "pipe", pairs)
        if tick < samples:
            skips_moved[tick] = lax.ppermute(sent_skip, "pipe", [(sections - 1, 0)])
    norms, outs, hiddens, dpres, mod_grads, firsts = kept
    total_rows = samples * rows

    mine_up, theirs_up = up_grad_call(
        scal,
        norms.reshape(slots, total_rows, width),
        dpres.reshape(slots, total_rows, hidden_width),
        order_x,
        condition_x,
        mod_grads,
    )
    other_up = lax.ppermute(theirs_up, "core", [(0, 1), (1, 0)])
    mine_down, theirs_down = down_grad_call(
        scal,
        hiddens.reshape(slots, total_rows, hidden_width),
        outs.reshape(slots, total_rows, width),
        skips.reshape(total_rows, width),
        firsts.reshape(total_rows, width),
        order_y,
        condition_y,
        mod_grads,
    )
    other_down = lax.ppermute(theirs_down, "core", [(0, 1), (1, 0)])

    sum_up = halved(lambda i: add(take(mine_up, i, 0), take(other_up, i, 0)), "x")
    sum_down = halved(lambda i: add(take(mine_down, i, 0), take(other_down, i, 0)), "y")
    block, part = width // 8, width // 32
    blocks = 2 * slots
    down_part = sum_down[:blocks].reshape(slots, 2, block, 2, width).transpose(1, 3, 0, 2, 4)
    down_part = down_part.reshape(4, slots * block, width)
    time_part = sum_down[blocks].reshape(4, part, 2, width).transpose(0, 2, 1, 3)
    skip_part = sum_down[blocks + 1, :, :width].reshape(4, part, width)
    down_part = jnp.concatenate(
        [down_part, time_part.reshape(4, 2 * part, width), skip_part], axis=1
    )
    up_part = sum_up.reshape(blocks + 2, 4, part, 2 * width)

    final_up = scattered(lambda i: take(up_part, i, 1), "y", F32)
    final_down = scattered(lambda i: take(down_part, i, 0), "x", F32)
    grad_up = final_up[:blocks].reshape(slots, 2, part, 2 * width).transpose(0, 2, 1, 3)
    grad_up = grad_up.reshape(slots, part, hidden_width)
    grad_down = final_down[: slots * block].reshape(slots, block, width)
    last_time = final_down[slots * block : slots * block + 2 * part].reshape(2, part, width)
    last_time = last_time.transpose(1, 0, 2).reshape(1, part, 2 * width)
    grad_time = jnp.concatenate([final_up[blocks:], last_time])
    grad_skip = final_down[slots * block + 2 * part :]
    return (grad_up[None], grad_down[None], grad_time[None], grad_skip[None])


def solution(mesh):
    split = Mesh(
        mesh.devices.reshape(4, 4, 2, mesh.devices.shape[1]), ("y", "x", "core", "pipe")
    )
    dp = ("y", "x", "core")
    placed = (
        P(dp, None, None),
        P(dp, None, None),
        P(dp),
        P("pipe"),
        P("pipe", None, None, None),
        P("pipe", None, None, None),
        P("pipe", None, None, None),
        P("pipe", None, None),
    )
    return jax.shard_map(
        per_device,
        mesh=split,
        in_specs=placed,
        out_specs=(
            P("pipe", None, dp, None),
            P("pipe", None, dp, None),
            P("pipe", None, dp, None),
            P("pipe", dp, None),
        ),
        check_vma=False,
    )
```

profile of v0, /device:TPU:0, one launch (start us, length us, event | category | flops | bytes accessed | tf_op | source)
XLA Modules:
  0.0 171.7 jit_solution(17240177448582753092)
XLA Ops:
  2.7 0.9 copy-done.1
  3.6 4.5 %section_forward_0.1 = (bf16[192,320]{1,0:T(8,128)(2,1)S(1)}, f32[3,3,192,320]{3,2,1,0:T(8,128)}, bf16[3,3,192,1280]{3,2,1,0:T(8,128)(2,1)}, bf16[3,192,320]{2,1,0:T(8,128)(2,1)}) custom-call(s32[4]{0:T(128)S(1)} %pad_add_fusion.refs_0_.scal, f32[3,3,640]{2,1,0:T(4,128)S(1)} %copy.156.refs_1_, bf16[3,192,320]{2,1,0:T(8,128)(2,1)} %refs_2_.26, ...), custom_call_target="tpu_custom_call" | custom-call | flops 943718400 | bytes 8000000 | tf_op jit(solution)/shard_map/section_forward_0/pallas_call | solution.py:173
  8.1 1.3 collective-permute-start
  9.4 4.5 %section_forward_1.1 = (bf16[192,320]{1,0:T(8,128)(2,1)S(1)}, f32[3,3,192,320]{3,2,1,0:T(8,128)}, bf16[3,3,192,1280]{3,2,1,0:T(8,128)(2,1)}, bf16[3,192,320]{2,1,0:T(8,128)(2,1)}) custom-call(s32[4]{0:T(128)S(1)} %pad_add_fusion.refs_0_.scal, f32[3,3,640]{2,1,0:T(4,128)S(1)} %copy.156.refs_1_, ...), custom_call_target="tpu_custom_call", output_to_operand_aliasing={{1}: (7, {}), {2}: (8, {}), {3}: (9, {})} | custom-call | flops 943718400 | bytes 8000000 | tf_op jit(solution)/shard_map/section_forward_1/pallas_call | solution.py:173
  13.9 1.3 collective-permute-start.2
  15.2 4.5 %section_forward_2.1 = (bf16[192,320]{1,0:T(8,128)(2,1)S(1)}, f32[3,3,192,320]{3,2,1,0:T(8,128)}, bf16[3,3,192,1280]{3,2,1,0:T(8,128)(2,1)}, bf16[3,192,320]{2,1,0:T(8,128)(2,1)}) custom-call(s32[4]{0:T(128)S(1)} %pad_add_fusion.refs_0_.scal, f32[3,3,640]{2,1,0:T(4,128)S(1)} %copy.156.refs_1_, ...), custom_call_target="tpu_custom_call", output_to_operand_aliasing={{1}: (7, {}), {2}: (8, {}), {3}: (9, {})} | custom-call | flops 943718400 | bytes 8000000 | tf_op jit(solution)/shard_map/section_forward_2/pallas_call | solution.py:173
  19.7 2.2 %collective-permute-start.1 = (bf16[192,320]{1,0:T(8,128)(2,1)S(1)}, bf16[192,320]{1,0:T(8,128)(2,1)S(1)}, u32[]{:S(2)}, u32[]{:S(2)}) collective-permute-start(bf16[192,320]{1,0:T(8,128)(2,1)S(1)} %get-tuple-element.113), channel_id=1, source_target_pairs={{0,1},{1,2},{4,5},{5,6},{8,9},{9,10},{12,13},{13,14},{16,17},{17,1... | collective-permute-start | bytes 368648 | tf_op jit(solution)/shard_map/ppermute | solution.py:710
  23.3 1.3 collective-permute-start.4
  26.0 1.3 collective-permute-start.9
  27.3 1.3 collective-permute-start.7
  32.5 1.1 collective-permute-done.7.refs_7_
  35.8 1.0 section_backward_1.1
  37.5 0.8 section_backward_2.1
  39.0 0.8 section_backward_3.1
  40.5 1.3 collective-permute-start.14
  42.6 1.3 collective-permute-start.13
  43.9 1.3 collective-permute-start.19
  45.2 1.3 collective-permute-start.17
  46.6 0.8 section_backward_5.1
  47.4 1.3 collective-permute-start.18
  48.7 31.1 %collective-permute-done.14.refs_9_ = bf16[192,320]{1,0:T(8,128)(2,1)S(1)} collective-permute-done((bf16[192,320]{1,0:T(8,128)(2,1)S(1)}, bf16[192,320]{1,0:T(8,128)(2,1)S(1)}, u32[]{:S(2)}, u32[]{:S(2)}) %collective-permute-start.14) | collective-permute-done | bytes 122912 | tf_op jit(solution)/shard_map/ppermute | solution.py:742
  79.8 7.1 %collective-permute-done.13.refs_3_ = bf16[192,320]{1,0:T(8,128)(2,1)S(1)} collective-permute-done((bf16[192,320]{1,0:T(8,128)(2,1)S(1)}, bf16[192,320]{1,0:T(8,128)(2,1)S(1)}, u32[]{:S(2)}, u32[]{:S(2)}) %collective-permute-start.13) | collective-permute-done | bytes 122912 | tf_op jit(solution)/shard_map/ppermute | solution.py:740
  86.9 5.8 %section_backward_6.1 = (bf16[192,320]{1,0:T(8,128)(2,1)S(1)}, bf16[192,320]{1,0:T(8,128)(2,1)}, bf16[3,3,192,320]{3,2,1,0:T(8,128)(2,1)}, bf16[3,3,192,320]{3,2...) custom-call(s32[4]{0:T(128)S(1)} %pad_add_fusion.refs_0_.scal, ...), custom_call_target="tpu_custom_call", output_to_operand_aliasing={{2}: (10, {}), {3}: (11, {}), {4}: (12, {}), {5}: (13, {}),... | custom-call | flops 943718400 | bytes 14000000 | tf_op jit(solution)/shard_map/section_backward_6/pallas_call | solution.py:390
  92.7 1.3 collective-permute-start.16
  94.1 0.8 copy.160.condition
  95.0 1.4 collective-permute-done.18.refs_3_
  96.4 5.8 %section_backward_7.1 = (bf16[192,320]{1,0:T(8,128)(2,1)}, bf16[192,320]{1,0:T(8,128)(2,1)}, bf16[3,3,192,320]{3,2,1,0:T(8,128)(2,1)}, bf16[3,3,192,320]{3,2,1,0...) custom-call(s32[4]{0:T(128)S(1)} %pad_add_fusion.refs_0_.scal, ...), custom_call_target="tpu_custom_call", output_to_operand_aliasing={{2}: (10, {}), {3}: (11, {}), {4}: (12, {}), {5}: (13, {}),... | custom-call | flops 943718400 | bytes 14000000 | tf_op jit(solution)/shard_map/section_backward_7/pallas_call | solution.py:390
  102.1 1.8 %collective-permute-done.16.refs_3_ = bf16[192,320]{1,0:T(8,128)(2,1)S(1)} collective-permute-done((bf16[192,320]{1,0:T(8,128)(2,1)S(1)}, bf16[192,320]{1,0:T(8,128)(2,1)S(1)}, u32[]{:S(2)}, u32[]{:S(2)}) %collective-permute-start.16) | collective-permute-done | bytes 122912 | tf_op jit(solution)/shard_map/ppermute | solution.py:740
  103.9 5.8 %section_backward_8.1 = (bf16[192,320]{1,0:T(8,128)(2,1)}, bf16[192,320]{1,0:T(8,128)(2,1)}, bf16[3,3,192,320]{3,2,1,0:T(8,128)(2,1)}, bf16[3,3,192,320]{3,2,1,0...) custom-call(s32[4]{0:T(128)S(1)} %pad_add_fusion.refs_0_.scal, ...), custom_call_target="tpu_custom_call", output_to_operand_aliasing={{2}: (10, {}), {3}: (11, {}), {4}: (12, {}), {5}: (13, {}),... | custom-call | flops 943718400 | bytes 14000000 | tf_op jit(solution)/shard_map/section_backward_8/pallas_call | solution.py:390
  110.3 7.0 %down_grad.1 = (bf16[4,8,40,640]{3,2,1,0:T(8,128)(2,1)}, bf16[4,8,40,640]{3,2,1,0:T(8,128)(2,1)}) custom-call(s32[4]{0:T(128)} %copy-done.4, bf16[3,576,1280]{2,1,0:T(8,128)(2,1)} %bitcast.165, bf16[3,576,320]{2,1,0:T(8,128)(2,1)} %bitcast.168, bf16[576,320]{1,0:T(8,128)(2,1)} %bitcast.170, bf16[576,320]{1,0:T(8,128)(2,1)} %bitcast.169, ...), custom_call_target="tpu_custom_call" | custom-call | flops 1415577600 | bytes 12000000 | tf_op jit(solution)/shard_map/down_grad/pallas_call | solution.py:581
  117.5 0.8 copy.157.condition
  118.3 7.0 %up_grad.1 = (bf16[4,8,40,640]{3,2,1,0:T(8,128)(2,1)}, bf16[4,8,40,640]{3,2,1,0:T(8,128)(2,1)}) custom-call(s32[4]{0:T(128)} %copy-done.4, bf16[3,576,320]{2,1,0:T(8,128)(2,1)} %bitcast.167, bf16[3,576,1280]{2,1,0:T(8,128)(2,1)} %bitcast.166, bf16[320,320]{1,0:T(8,128)(2,1)} %constant.109.clone.order, f32[320,3]{1,0:T(8,128)} %copy.157.condition, ...), custom_call_target="tpu_custom_call" | custom-call | flops 1415577600 | bytes 12000000 | tf_op jit(solution)/shard_map/up_grad/pallas_call | solution.py:487
  125.8 2.3 %add_convert_fusion.3 = (bf16[1,8,40,640]{3,2,1,0:T(8,128)(2,1)S(1)}, bf16[1,8,40,640]{3,2,1,0:T(8,128)(2,1)S(1)}, bf16[1,8,40,640]{3,2,1,0:T(8,128)(2,1)S(1)}, bf16[1,8,40,640]{3,2,1,0:T(8,128)(2,1)S(1)}) fusion(bf16[4,8,40,640]{3,2,1,0:T(8,128)(2,1)} %collective-permute-done.28, s32[]{:T(128)S(6)} %select_n.55, ...), kind=kLoop, calls=%fused_computation.7 | loop fusion | flops 3276800 | bytes 4915216 | tf_op jit(solution)/shard_map/convert_element_type | solution.py:661
  128.2 3.4 %collective-permute-start.29 = (bf16[8,40,640]{2,1,0:T(8,128)(2,1)S(1)}, bf16[8,40,640]{2,1,0:T(8,128)(2,1)S(1)}, u32[]{:S(2)}, u32[]{:S(2)}) collective-permute-start(bf16[8,40,640]{2,1,0:T(8,128)(2,1)S(1)} %pad_maximum_fusion.4), channel_id=1, source_target_pairs={{0,96},{32,0},{64,32},{96,64},{1,97},{33,1},{65,33},{97,65},{2,98}... | collective-permute-start | bytes 1228808 | tf_op jit(solution)/shard_map/ppermute | solution.py:648
  132.4 2.8 %collective-permute-start.21 = (bf16[8,40,640]{2,1,0:T(8,128)(2,1)S(1)}, bf16[8,40,640]{2,1,0:T(8,128)(2,1)S(1)}, u32[]{:S(2)}, u32[]{:S(2)}) collective-permute-start(bf16[8,40,640]{2,1,0:T(8,128)(2,1)S(1)} %pad_maximum_fusion.1), channel_id=1, source_target_pairs={{0,24},{8,0},{16,8},{24,16},{1,25},{9,1},{17,9},{25,17},{2,26},{10... | collective-permute-start | bytes 1228808 | tf_op jit(solution)/shard_map/ppermute | solution.py:648
  135.4 5.2 %collective-permute-done.29 = bf16[8,40,640]{2,1,0:T(8,128)(2,1)S(1)} collective-permute-done((bf16[8,40,640]{2,1,0:T(8,128)(2,1)S(1)}, bf16[8,40,640]{2,1,0:T(8,128)(2,1)S(1)}, u32[]{:S(2)}, u32[]{:S(2)}) %collective-permute-start.29) | collective-permute-done | bytes 409632 | tf_op jit(solution)/shard_map/ppermute | solution.py:648
  140.7 3.8 %collective-permute-start.32 = (bf16[4,40,640]{2,1,0:T(8,128)(2,1)S(1)}, bf16[4,40,640]{2,1,0:T(8,128)(2,1)S(1)}, u32[]{:S(2)}, u32[]{:S(2)}) collective-permute-start(bf16[4,40,640]{2,1,0:T(8,128)(2,1)S(1)} %fusion.2), channel_id=1, source_target_pairs={{0,96},{32,0},{64,32},{96,64},{1,97},{33,1},{65,33},{97,65},{2,98}... | collective-permute-start | bytes 614408 | tf_op jit(solution)/shard_map/ppermute | solution.py:651
  145.3 3.0 %collective-permute-start.24 = (bf16[4,40,640]{2,1,0:T(8,128)(2,1)}, bf16[4,40,640]{2,1,0:T(8,128)(2,1)S(1)}, u32[]{:S(2)}, u32[]{:S(2)}) collective-permute-start(bf16[4,40,640]{2,1,0:T(8,128)(2,1)} %fusion.8), channel_id=1, source_target_pairs={{0,24},{8,0},{16,8},{24,16},{1,25},{9,1},{17,9},{25,17},{2,26},{10... | collective-permute-start | bytes 614408 | tf_op jit(solution)/shard_map/ppermute | solution.py:651
  148.4 0.8 fusion.11
  149.2 2.5 %collective-permute-done.31 = bf16[4,40,640]{2,1,0:T(8,128)(2,1)S(1)} collective-permute-done((bf16[4,40,640]{2,1,0:T(8,128)(2,1)S(1)}, bf16[4,40,640]{2,1,0:T(8,128)(2,1)S(1)}, u32[]{:S(2)}, u32[]{:S(2)}) %collective-permute-start.31) | collective-permute-done | bytes 204832 | tf_op jit(solution)/shard_map/ppermute | solution.py:650
  152.7 3.1 %collective-permute-start.33 = (bf16[150,320]{1,0:T(8,128)(2,1)S(1)}, bf16[150,320]{1,0:T(8,128)(2,1)S(1)}, u32[]{:S(2)}, u32[]{:S(2)}) collective-permute-start(bf16[150,320]{1,0:T(8,128)(2,1)S(1)} %get-tuple-element.224), channel_id=1, source_target_pairs={{0,16},{8,24},{16,0},{24,8},{1,17},{9,25},{17,1},{25,9},{2,18},{10... | collective-permute-start | bytes 288008 | tf_op jit(solution)/shard_map/ppermute | solution.py:633
  156.4 2.7 %collective-permute-start.35 = (bf16[150,320]{1,0:T(8,128)(2,1)S(1)}, bf16[150,320]{1,0:T(8,128)(2,1)S(1)}, u32[]{:S(2)}, u32[]{:S(2)}) collective-permute-start(bf16[150,320]{1,0:T(8,128)(2,1)S(1)} %get-tuple-element.225), channel_id=1, source_target_pairs={{0,24},{8,0},{16,8},{24,16},{1,25},{9,1},{17,9},{25,17},{2,26},{10... | collective-permute-start | bytes 288008 | tf_op jit(solution)/shard_map/ppermute | solution.py:633
  159.0 1.2 fusion.13
  160.4 2.7 %collective-permute-start.25 = (bf16[8,10,640]{2,0,1:T(8,128)(2,1)S(1)}, bf16[8,10,640]{2,0,1:T(8,128)(2,1)S(1)}, u32[]{:S(2)}, u32[]{:S(2)}) collective-permute-start(bf16[8,10,640]{2,0,1:T(8,128)(2,1)S(1)} %get-tuple-element.231), channel_id=1, source_target_pairs={{0,64},{32,96},{64,0},{96,32},{1,65},{33,97},{65,1},{97,33},{2,66}... | collective-permute-start | bytes 307208 | tf_op jit(solution)/shard_map/ppermute | solution.py:633
  163.1 2.0 %collective-permute-start.26 = (bf16[8,10,640]{2,0,1:T(8,128)(2,1)S(1)}, bf16[8,10,640]{2,0,1:T(8,128)(2,1)S(1)}, u32[]{:S(2)}, u32[]{:S(2)}) collective-permute-start(bf16[8,10,640]{2,0,1:T(8,128)(2,1)S(1)} %get-tuple-element.233), channel_id=1, source_target_pairs={{0,32},{32,64},{64,96},{96,0},{1,33},{33,65},{65,97},{97,1},{2,34}... | collective-permute-start | bytes 307208 | tf_op jit(solution)/shard_map/ppermute | solution.py:633
  165.1 1.2 collective-permute-start.27
  167.9 1.1 collective-permute-done.26
  170.8 0.9 broadcast_in_dim_reshape.6
  (121 shorter events, 21.0 us)
Async XLA Ops:
  0.6 1.6 copy-start
  2.7 101.2 %copy-start.4 = (s32[4]{0:T(128)}, s32[4]{0:T(128)S(1)}, u32[]{:S(2)}) copy-start(s32[4]{0:T(128)S(1)} %pad_add_fusion.refs_0_.scal) | copy-start | bytes 52
  2.7 0.9 copy-start.1
  8.1 7.1 %collective-permute-start = (bf16[192,320]{1,0:T(8,128)(2,1)S(1)}, bf16[192,320]{1,0:T(8,128)(2,1)S(1)}, u32[]{:S(2)}, u32[]{:S(2)}) collective-permute-start(bf16[192,320]{1,0:T(8,128)(2,1)S(1)} %get-tuple-element.106), channel_id=1, source_target_pairs={{0,1},{4,5},{8,9},{12,13},{16,17},{20,21},{24,25},{28,29},{32,33},... | collective-permute-start | bytes 368648 | tf_op jit(solution)/shard_map/ppermute | solution.py:710
  9.4 5.8 %copy-start.2 = (bf16[1,320,320]{2,1,0:T(8,128)(2,1)S(1)}, bf16[1,320,320]{2,1,0:T(8,128)(2,1)}, u32[]{:S(2)}) copy-start(bf16[1,320,320]{2,1,0:T(8,128)(2,1)} %param.17) | copy-start | bytes 614404
  13.9 8.0 %collective-permute-start.2 = (bf16[192,320]{1,0:T(8,128)(2,1)S(1)}, bf16[192,320]{1,0:T(8,128)(2,1)S(1)}, u32[]{:S(2)}, u32[]{:S(2)}) collective-permute-start(bf16[192,320]{1,0:T(8,128)(2,1)S(1)} %get-tuple-element.114), channel_id=1, source_target_pairs={{0,1},{4,5},{8,9},{12,13},{16,17},{20,21},{24,25},{28,29},{32,33},... | collective-permute-start | bytes 368648 | tf_op jit(solution)/shard_map/ppermute | solution.py:710
  19.7 4.9 %collective-permute-start.1 = (bf16[192,320]{1,0:T(8,128)(2,1)S(1)}, bf16[192,320]{1,0:T(8,128)(2,1)S(1)}, u32[]{:S(2)}, u32[]{:S(2)}) collective-permute-start(bf16[192,320]{1,0:T(8,128)(2,1)S(1)} %get-tuple-element.113), channel_id=1, source_target_pairs={{0,1},{1,2},{4,5},{5,6},{8,9},{9,10},{12,13},{13,14},{16,17},{17,1... | collective-permute-start | bytes 368648 | tf_op jit(solution)/shard_map/ppermute | solution.py:710
  22.6 6.0 %collective-permute-start.5 = (bf16[192,320]{1,0:T(8,128)(2,1)S(1)}, bf16[192,320]{1,0:T(8,128)(2,1)S(1)}, u32[]{:S(2)}, u32[]{:S(2)}) collective-permute-start(bf16[192,320]{1,0:T(8,128)(2,1)S(1)} %get-tuple-element.122), channel_id=1, source_target_pairs={{1,2},{5,6},{9,10},{13,14},{17,18},{21,22},{25,26},{29,30},{33,34}... | collective-permute-start | bytes 368648 | tf_op jit(solution)/shard_map/ppermute | solution.py:710
  23.3 6.7 %collective-permute-start.4 = (bf16[192,320]{1,0:T(8,128)(2,1)S(1)}, bf16[192,320]{1,0:T(8,128)(2,1)S(1)}, u32[]{:S(2)}, u32[]{:S(2)}) collective-permute-start(bf16[192,320]{1,0:T(8,128)(2,1)S(1)} %get-tuple-element.106), channel_id=1, source_target_pairs={{0,3},{4,7},{8,11},{12,15},{16,19},{20,23},{24,27},{28,31},{32,35}... | collective-permute-start | bytes 368648 | tf_op jit(solution)/shard_map/ppermute | solution.py:712
  25.3 4.7 %collective-permute-start.3 = (bf16[192,320]{1,0:T(8,128)(2,1)S(1)}, bf16[192,320]{1,0:T(8,128)(2,1)S(1)}, u32[]{:S(2)}, u32[]{:S(2)}) collective-permute-start(bf16[192,320]{1,0:T(8,128)(2,1)S(1)} %get-tuple-element.121), channel_id=1, source_target_pairs={{1,2},{2,3},{5,6},{6,7},{9,10},{10,11},{13,14},{14,15},{17,18},{18... | collective-permute-start | bytes 368648 | tf_op jit(solution)/shard_map/ppermute | solution.py:710
  26.0 5.8 %collective-permute-start.9 = (bf16[192,320]{1,0:T(8,128)(2,1)S(1)}, bf16[192,320]{1,0:T(8,128)(2,1)S(1)}, u32[]{:S(2)}, u32[]{:S(2)}) collective-permute-start(bf16[192,320]{1,0:T(8,128)(2,1)S(1)} %get-tuple-element.114), channel_id=1, source_target_pairs={{0,3},{4,7},{8,11},{12,15},{16,19},{20,23},{24,27},{28,31},{32,35}... | collective-permute-start | bytes 368648 | tf_op jit(solution)/shard_map/ppermute | solution.py:712
  27.3 6.3 %collective-permute-start.7 = (bf16[192,320]{1,0:T(8,128)(2,1)S(1)}, bf16[192,320]{1,0:T(8,128)(2,1)S(1)}, u32[]{:S(2)}, u32[]{:S(2)}) collective-permute-start(bf16[192,320]{1,0:T(8,128)(2,1)S(1)} %get-tuple-element.113), channel_id=1, source_target_pairs={{0,3},{4,7},{8,11},{12,15},{16,19},{20,23},{24,27},{28,31},{32,35}... | collective-permute-start | bytes 368648 | tf_op jit(solution)/shard_map/ppermute | solution.py:712
  29.4 2.5 %collective-permute-start.8 = (bf16[192,320]{1,0:T(8,128)(2,1)S(1)}, bf16[192,320]{1,0:T(8,128)(2,1)S(1)}, u32[]{:S(2)}, u32[]{:S(2)}) collective-permute-start(bf16[192,320]{1,0:T(8,128)(2,1)S(1)} %get-tuple-element.130), channel_id=1, source_target_pairs={{2,3},{6,7},{10,11},{14,15},{18,19},{22,23},{26,27},{30,31},{34,35... | collective-permute-start | bytes 368648 | tf_op jit(solution)/shard_map/ppermute | solution.py:710
  30.8 2.8 %collective-permute-start.6 = (bf16[192,320]{1,0:T(8,128)(2,1)S(1)}, bf16[192,320]{1,0:T(8,128)(2,1)S(1)}, u32[]{:S(2)}, u32[]{:S(2)}) collective-permute-start(bf16[192,320]{1,0:T(8,128)(2,1)S(1)} %get-tuple-element.129), channel_id=1, source_target_pairs={{2,3},{6,7},{10,11},{14,15},{18,19},{22,23},{26,27},{30,31},{34,35... | collective-permute-start | bytes 368648 | tf_op jit(solution)/shard_map/ppermute | solution.py:710
  35.1 2.4 %collective-permute-start.10 = (bf16[192,320]{1,0:T(8,128)(2,1)S(1)}, bf16[192,320]{1,0:T(8,128)(2,1)S(1)}, u32[]{:S(2)}, u32[]{:S(2)}) collective-permute-start(bf16[192,320]{1,0:T(8,128)(2,1)S(1)} %get-tuple-element.139), channel_id=1, source_target_pairs={{3,2},{7,6},{11,10},{15,14},{19,18},{23,22},{27,26},{31,30},{35,34... | collective-permute-start | bytes 368648 | tf_op jit(solution)/shard_map/ppermute | solution.py:740
  36.8 2.2 %collective-permute-start.12 = (bf16[192,320]{1,0:T(8,128)(2,1)S(1)}, bf16[192,320]{1,0:T(8,128)(2,1)S(1)}, u32[]{:S(2)}, u32[]{:S(2)}) collective-permute-start(bf16[192,320]{1,0:T(8,128)(2,1)S(1)} %get-tuple-element.153), channel_id=1, source_target_pairs={{3,2},{7,6},{11,10},{15,14},{19,18},{23,22},{27,26},{31,30},{35,34... | collective-permute-start | bytes 368648 | tf_op jit(solution)/shard_map/ppermute | solution.py:740
  38.3 3.5 %collective-permute-start.11 = (bf16[192,320]{1,0:T(8,128)(2,1)S(1)}, bf16[192,320]{1,0:T(8,128)(2,1)S(1)}, u32[]{:S(2)}, u32[]{:S(2)}) collective-permute-start(bf16[192,320]{1,0:T(8,128)(2,1)S(1)} %get-tuple-element.152), channel_id=1, source_target_pairs={{2,1},{3,2},{6,5},{7,6},{10,9},{11,10},{14,13},{15,14},{18,17},{19... | collective-permute-start | bytes 368648 | tf_op jit(solution)/shard_map/ppermute | solution.py:740
  39.8 6.7 %collective-permute-start.15 = (bf16[192,320]{1,0:T(8,128)(2,1)S(1)}, bf16[192,320]{1,0:T(8,128)(2,1)S(1)}, u32[]{:S(2)}, u32[]{:S(2)}) collective-permute-start(bf16[192,320]{1,0:T(8,128)(2,1)S(1)} %get-tuple-element.168), channel_id=1, source_target_pairs={{2,1},{6,5},{10,9},{14,13},{18,17},{22,21},{26,25},{30,29},{34,33}... | collective-permute-start | bytes 368648 | tf_op jit(solution)/shard_map/ppermute | solution.py:740
  40.5 39.3 %collective-permute-start.14 = (bf16[192,320]{1,0:T(8,128)(2,1)S(1)}, bf16[192,320]{1,0:T(8,128)(2,1)S(1)}, u32[]{:S(2)}, u32[]{:S(2)}) collective-permute-start(bf16[192,320]{1,0:T(8,128)(2,1)S(1)} %get-tuple-element.167), channel_id=1, source_target_pairs={{3,0},{7,4},{11,8},{15,12},{19,16},{23,20},{27,24},{31,28},{35,32}... | collective-permute-start | bytes 368648 | tf_op jit(solution)/shard_map/ppermute | solution.py:742
  42.6 44.3 %collective-permute-start.13 = (bf16[192,320]{1,0:T(8,128)(2,1)S(1)}, bf16[192,320]{1,0:T(8,128)(2,1)S(1)}, u32[]{:S(2)}, u32[]{:S(2)}) collective-permute-start(bf16[192,320]{1,0:T(8,128)(2,1)S(1)} %get-tuple-element.166), channel_id=1, source_target_pairs={{1,0},{2,1},{5,4},{6,5},{9,8},{10,9},{13,12},{14,13},{17,16},{18,1... | collective-permute-start | bytes 368648 | tf_op jit(solution)/shard_map/ppermute | solution.py:740
  43.9 51.0 %collective-permute-start.19 = (bf16[192,320]{1,0:T(8,128)(2,1)S(1)}, bf16[192,320]{1,0:T(8,128)(2,1)S(1)}, u32[]{:S(2)}, u32[]{:S(2)}) collective-permute-start(bf16[192,320]{1,0:T(8,128)(2,1)S(1)} %get-tuple-element.184), channel_id=1, source_target_pairs={{3,0},{7,4},{11,8},{15,12},{19,16},{23,20},{27,24},{31,28},{35,32}... | collective-permute-start | bytes 368648 | tf_op jit(solution)/shard_map/ppermute | solution.py:742
  45.2 56.9 %collective-permute-start.17 = (bf16[192,320]{1,0:T(8,128)(2,1)S(1)}, bf16[192,320]{1,0:T(8,128)(2,1)S(1)}, u32[]{:S(2)}, u32[]{:S(2)}) collective-permute-start(bf16[192,320]{1,0:T(8,128)(2,1)S(1)} %get-tuple-element.182), channel_id=1, source_target_pairs={{3,0},{7,4},{11,8},{15,12},{19,16},{23,20},{27,24},{31,28},{35,32}... | collective-permute-start | bytes 368648 | tf_op jit(solution)/shard_map/ppermute | solution.py:742
  47.4 49.0 %collective-permute-start.18 = (bf16[192,320]{1,0:T(8,128)(2,1)S(1)}, bf16[192,320]{1,0:T(8,128)(2,1)S(1)}, u32[]{:S(2)}, u32[]{:S(2)}) collective-permute-start(bf16[192,320]{1,0:T(8,128)(2,1)S(1)} %get-tuple-element.183), channel_id=1, source_target_pairs={{1,0},{5,4},{9,8},{13,12},{17,16},{21,20},{25,24},{29,28},{33,32},... | collective-permute-start | bytes 368648 | tf_op jit(solution)/shard_map/ppermute | solution.py:740
  86.9 7.1 %copy-start.6 = (bf16[320,320]{1,0:T(8,128)(2,1)S(1)}, bf16[320,320]{1,0:T(8,128)(2,1)}, u32[]{:S(2)}) copy-start(bf16[320,320]{1,0:T(8,128)(2,1)} %constant.110.clone.order) | copy-start | bytes 614404
  92.7 11.2 %collective-permute-start.16 = (bf16[192,320]{1,0:T(8,128)(2,1)S(1)}, bf16[192,320]{1,0:T(8,128)(2,1)S(1)}, u32[]{:S(2)}, u32[]{:S(2)}) collective-permute-start(bf16[192,320]{1,0:T(8,128)(2,1)S(1)} %get-tuple-element.181), channel_id=1, source_target_pairs={{1,0},{5,4},{9,8},{13,12},{17,16},{21,20},{25,24},{29,28},{33,32},... | collective-permute-start | bytes 368648 | tf_op jit(solution)/shard_map/ppermute | solution.py:740
  109.7 0.6 copy-start.3
  110.3 7.0 %copy-start.7 = (bf16[320,320]{1,0:T(8,128)(2,1)S(1)}, bf16[320,320]{1,0:T(8,128)(2,1)}, u32[]{:S(2)}) copy-start(bf16[320,320]{1,0:T(8,128)(2,1)} %constant.109.clone.order) | copy-start | bytes 614404
  117.3 8.5 %collective-permute-start.28 = (bf16[4,8,40,640]{3,2,1,0:T(8,128)(2,1)}, bf16[4,8,40,640]{3,2,1,0:T(8,128)(2,1)}, u32[]{:S(2)}, u32[]{:S(2)}) collective-permute-start(bf16[4,8,40,640]{3,2,1,0:T(8,128)(2,1)} %get-tuple-element.207), channel_id=1, source_target_pairs={{0,4},{4,0},{1,5},{5,1},{2,6},{6,2},{3,7},{7,3},{8,12},{12,8},{9,1... | collective-permute-start | bytes 4915208 | tf_op jit(solution)/shard_map/ppermute | solution.py:765
  125.3 6.5 %collective-permute-start.20 = (bf16[4,8,40,640]{3,2,1,0:T(8,128)(2,1)}, bf16[4,8,40,640]{3,2,1,0:T(8,128)(2,1)S(1)}, u32[]{:S(2)}, u32[]{:S(2)}) collective-permute-start(bf16[4,8,40,640]{3,2,1,0:T(8,128)(2,1)} %get-tuple-element.201), channel_id=1, source_target_pairs={{0,4},{4,0},{1,5},{5,1},{2,6},{6,2},{3,7},{7,3},{8,12},{12,8},{9,1... | collective-permute-start | bytes 4915208 | tf_op jit(solution)/shard_map/ppermute | solution.py:754
  128.1 3.7 %copy-start.5 = (bf16[4,8,40,640]{3,2,1,0:T(8,128)(2,1)S(1)}, bf16[4,8,40,640]{3,2,1,0:T(8,128)(2,1)}, u32[]{:S(2)}) copy-start(bf16[4,8,40,640]{3,2,1,0:T(8,128)(2,1)} %get-tuple-element.200) | copy-start | bytes 4915204
  128.2 12.4 %collective-permute-start.29 = (bf16[8,40,640]{2,1,0:T(8,128)(2,1)S(1)}, bf16[8,40,640]{2,1,0:T(8,128)(2,1)S(1)}, u32[]{:S(2)}, u32[]{:S(2)}) collective-permute-start(bf16[8,40,640]{2,1,0:T(8,128)(2,1)S(1)} %pad_maximum_fusion.4), channel_id=1, source_target_pairs={{0,96},{32,0},{64,32},{96,64},{1,97},{33,1},{65,33},{97,65},{2,98}... | collective-permute-start | bytes 1228808 | tf_op jit(solution)/shard_map/ppermute | solution.py:648
  131.7 12.7 %collective-permute-start.30 = (bf16[8,40,640]{2,1,0:T(8,128)(2,1)S(1)}, bf16[8,40,640]{2,1,0:T(8,128)(2,1)S(1)}, u32[]{:S(2)}, u32[]{:S(2)}) collective-permute-start(bf16[8,40,640]{2,1,0:T(8,128)(2,1)S(1)} %pad_maximum_fusion.5), channel_id=1, source_target_pairs={{0,32},{32,64},{64,96},{96,0},{1,33},{33,65},{65,97},{97,1},{2,34}... | collective-permute-start | bytes 1228808 | tf_op jit(solution)/shard_map/ppermute | solution.py:647
  132.4 12.2 %collective-permute-start.21 = (bf16[8,40,640]{2,1,0:T(8,128)(2,1)S(1)}, bf16[8,40,640]{2,1,0:T(8,128)(2,1)S(1)}, u32[]{:S(2)}, u32[]{:S(2)}) collective-permute-start(bf16[8,40,640]{2,1,0:T(8,128)(2,1)S(1)} %pad_maximum_fusion.1), channel_id=1, source_target_pairs={{0,24},{8,0},{16,8},{24,16},{1,25},{9,1},{17,9},{25,17},{2,26},{10... | collective-permute-start | bytes 1228808 | tf_op jit(solution)/shard_map/ppermute | solution.py:648
  135.3 13.1 %collective-permute-start.22 = (bf16[8,40,640]{2,1,0:T(8,128)(2,1)S(1)}, bf16[8,40,640]{2,1,0:T(8,128)(2,1)S(1)}, u32[]{:S(2)}, u32[]{:S(2)}) collective-permute-start(bf16[8,40,640]{2,1,0:T(8,128)(2,1)S(1)} %pad_maximum_fusion.2), channel_id=1, source_target_pairs={{0,8},{8,16},{16,24},{24,0},{1,9},{9,17},{17,25},{25,1},{2,10},{10... | collective-permute-start | bytes 1228808 | tf_op jit(solution)/shard_map/ppermute | solution.py:647
  140.7 8.6 %collective-permute-start.32 = (bf16[4,40,640]{2,1,0:T(8,128)(2,1)S(1)}, bf16[4,40,640]{2,1,0:T(8,128)(2,1)S(1)}, u32[]{:S(2)}, u32[]{:S(2)}) collective-permute-start(bf16[4,40,640]{2,1,0:T(8,128)(2,1)S(1)} %fusion.2), channel_id=1, source_target_pairs={{0,96},{32,0},{64,32},{96,64},{1,97},{33,1},{65,33},{97,65},{2,98}... | collective-permute-start | bytes 614408 | tf_op jit(solution)/shard_map/ppermute | solution.py:651
  144.5 7.2 %collective-permute-start.31 = (bf16[4,40,640]{2,1,0:T(8,128)(2,1)S(1)}, bf16[4,40,640]{2,1,0:T(8,128)(2,1)S(1)}, u32[]{:S(2)}, u32[]{:S(2)}) collective-permute-start(bf16[4,40,640]{2,1,0:T(8,128)(2,1)S(1)} %fusion.5), channel_id=1, source_target_pairs={{0,32},{32,64},{64,96},{96,0},{1,33},{33,65},{65,97},{97,1},{2,34}... | collective-permute-start | bytes 614408 | tf_op jit(solution)/shard_map/ppermute | solution.py:650
  145.3 13.7 %collective-permute-start.24 = (bf16[4,40,640]{2,1,0:T(8,128)(2,1)}, bf16[4,40,640]{2,1,0:T(8,128)(2,1)S(1)}, u32[]{:S(2)}, u32[]{:S(2)}) collective-permute-start(bf16[4,40,640]{2,1,0:T(8,128)(2,1)} %fusion.8), channel_id=1, source_target_pairs={{0,24},{8,0},{16,8},{24,16},{1,25},{9,1},{17,9},{25,17},{2,26},{10... | collective-permute-start | bytes 614408 | tf_op jit(solution)/shard_map/ppermute | solution.py:651
  148.4 3.3 %copy-start.8 = (bf16[8,40,640]{2,1,0:T(8,128)(2,1)}, bf16[8,40,640]{2,1,0:T(8,128)(2,1)S(1)}, u32[]{:S(2)}) copy-start(bf16[8,40,640]{2,1,0:T(8,128)(2,1)S(1)} %collective-permute-done.22) | copy-start | bytes 1228804
  149.2 9.8 %collective-permute-start.23 = (bf16[4,40,640]{2,1,0:T(8,128)(2,1)}, bf16[4,40,640]{2,1,0:T(8,128)(2,1)}, u32[]{:S(2)}, u32[]{:S(2)}) collective-permute-start(bf16[4,40,640]{2,1,0:T(8,128)(2,1)} %fusion.11), channel_id=1, source_target_pairs={{0,8},{8,16},{16,24},{24,0},{1,9},{9,17},{17,25},{25,1},{2,10},{10... | collective-permute-start | bytes 614408 | tf_op jit(solution)/shard_map/ppermute | solution.py:650
  152.7 12.5 %collective-permute-start.33 = (bf16[150,320]{1,0:T(8,128)(2,1)S(1)}, bf16[150,320]{1,0:T(8,128)(2,1)S(1)}, u32[]{:S(2)}, u32[]{:S(2)}) collective-permute-start(bf16[150,320]{1,0:T(8,128)(2,1)S(1)} %get-tuple-element.224), channel_id=1, source_target_pairs={{0,16},{8,24},{16,0},{24,8},{1,17},{9,25},{17,1},{25,9},{2,18},{10... | collective-permute-start | bytes 288008 | tf_op jit(solution)/shard_map/ppermute | solution.py:633
  155.8 10.6 %collective-permute-start.34 = (bf16[150,320]{1,0:T(8,128)(2,1)S(1)}, bf16[150,320]{1,0:T(8,128)(2,1)S(1)}, u32[]{:S(2)}, u32[]{:S(2)}) collective-permute-start(bf16[150,320]{1,0:T(8,128)(2,1)S(1)} %get-tuple-element.226), channel_id=1, source_target_pairs={{0,8},{8,16},{16,24},{24,0},{1,9},{9,17},{17,25},{25,1},{2,10},{10... | collective-permute-start | bytes 288008 | tf_op jit(solution)/shard_map/ppermute | solution.py:633
  156.4 10.0 %collective-permute-start.35 = (bf16[150,320]{1,0:T(8,128)(2,1)S(1)}, bf16[150,320]{1,0:T(8,128)(2,1)S(1)}, u32[]{:S(2)}, u32[]{:S(2)}) collective-permute-start(bf16[150,320]{1,0:T(8,128)(2,1)S(1)} %get-tuple-element.225), channel_id=1, source_target_pairs={{0,24},{8,0},{16,8},{24,16},{1,25},{9,1},{17,9},{25,17},{2,26},{10... | collective-permute-start | bytes 288008 | tf_op jit(solution)/shard_map/ppermute | solution.py:633
  160.4 7.5 %collective-permute-start.25 = (bf16[8,10,640]{2,0,1:T(8,128)(2,1)S(1)}, bf16[8,10,640]{2,0,1:T(8,128)(2,1)S(1)}, u32[]{:S(2)}, u32[]{:S(2)}) collective-permute-start(bf16[8,10,640]{2,0,1:T(8,128)(2,1)S(1)} %get-tuple-element.231), channel_id=1, source_target_pairs={{0,64},{32,96},{64,0},{96,32},{1,65},{33,97},{65,1},{97,33},{2,66}... | collective-permute-start | bytes 307208 | tf_op jit(solution)/shard_map/ppermute | solution.py:633
  163.1 5.9 %collective-permute-start.26 = (bf16[8,10,640]{2,0,1:T(8,128)(2,1)S(1)}, bf16[8,10,640]{2,0,1:T(8,128)(2,1)S(1)}, u32[]{:S(2)}, u32[]{:S(2)}) collective-permute-start(bf16[8,10,640]{2,0,1:T(8,128)(2,1)S(1)} %get-tuple-element.233), channel_id=1, source_target_pairs={{0,32},{32,64},{64,96},{96,0},{1,33},{33,65},{65,97},{97,1},{2,34}... | collective-permute-start | bytes 307208 | tf_op jit(solution)/shard_map/ppermute | solution.py:633
  165.1 4.7 %collective-permute-start.27 = (bf16[8,10,640]{2,0,1:T(8,128)(2,1)S(1)}, bf16[8,10,640]{2,0,1:T(8,128)(2,1)S(1)}, u32[]{:S(2)}, u32[]{:S(2)}) collective-permute-start(bf16[8,10,640]{2,0,1:T(8,128)(2,1)S(1)} %get-tuple-element.232), channel_id=1, source_target_pairs={{0,96},{32,0},{64,32},{96,64},{1,97},{33,1},{65,33},{97,65},{2,98}... | collective-permute-start | bytes 307208 | tf_op jit(solution)/shard_map/ppermute | solution.py:633
where the time goes:
time: 173 us; the launch traced here: 172 us
  Pallas kernels  54 us (31%)
  waiting for transfers between devices  52.5 us (30%)
  starting transfers between devices  47.9 us (28%)
  local copies, waits for them, and re-layouts  7.29 us (4%)
  other arithmetic  7.23 us (4%)
  between operations  2.19 us (1%)
    ppermute x3, waiting for transfers between devices, per_device(): skips_moved[tick] = lax.ppermute(sent_skip, 'pipe', [(sections - 1, 0)])  31.1 us
    pallas_call x9, Pallas kernels, backward_call(): pl.pallas_call(functools.partial(backward_kernel, tick, saved is not None...  22.4 us
    pallas_call x9, Pallas kernels, forward_call(): pl.pallas_call(functools.partial(forward_kernel, tick, saved is not None,...  17.6 us
    ppermute x14, starting transfers between devices, per_device(): moved[tick] = lax.ppermute(sent, 'pipe', pairs)  14 us
    ppermute x6, starting transfers between devices, scattered(): lax.ppermute(pieces(lax.rem(index + d, size)), axis, shifted(size, d))  12.3 us
    ppermute x14, waiting for transfers between devices, per_device(): moved[tick] = lax.ppermute(sent, 'pipe', pairs)  10.3 us
    pallas_call x1, Pallas kernels, down_grad_call(): pl.pallas_call(down_grad_kernel, grid=(slots + 1,), out_shape=(shape, sha...  7.02 us
    pallas_call x1, Pallas kernels, up_grad_call(): pl.pallas_call(up_grad_kernel, grid=(slots + 1,), out_shape=(shape, shape...  7.01 us
  transfers between devices with their start and end apart: 36, of which 10 were waited for; matrix products, arithmetic and copies ran while one was open for 6% of the time, Pallas kernels for 21%

commit v1 on v0

v1 whole, which is shorter than its diff:
```python
import functools
import math

import jax
import jax.numpy as jnp
import ml_dtypes
import numpy as np
from jax import lax
from jax.experimental import pallas as pl
from jax.experimental.pallas import tpu as pltpu
from jax.sharding import Mesh
from jax.sharding import PartitionSpec as P

EPSILON = 1e-06
BF16 = jnp.bfloat16
F32 = jnp.float32
CHUNK = 256
SECTION_VMEM = 53 * 1024 * 1024
GRAD_VMEM = 56 * 1024 * 1024
ANY = pl.BlockSpec(memory_space=pl.ANY)
VMEM = pl.BlockSpec(memory_space=pltpu.VMEM)
SMEM = pl.BlockSpec(memory_space=pltpu.SMEM)
NT = (((1,), (1,)), ((), ()))
TN = (((0,), (0,)), ((), ()))


def embedding(timesteps, halfway):
    frequency = jnp.exp(-math.log(10000.0) * jnp.arange(halfway, dtype=F32) / halfway)
    angles = timesteps.astype(F32)[..., None] * frequency
    return jnp.concatenate([jnp.sin(angles), jnp.cos(angles)], axis=-1)


def nt_dot(left, right):
    return lax.dot_general(left, right, NT, preferred_element_type=F32)


def sigmoid(value):
    return 0.5 * jnp.tanh(0.5 * value) + 0.5


def backward_layers(count, sample, slots, width, buffers, targets, sems, base, loads):
    modv, upv, downv, statev, prev, acc, nv, ov, hidv, dpv, mgv, fv = buffers
    norms, outs, hiddens, dpres, mod_grads, firsts = targets
    hidden_width = upv.shape[2]

    def saves(j):
        pairs = (
            (nv.at[j], norms.at[j, sample]),
            (ov.at[j], outs.at[j, sample]),
            (hidv.at[j], hiddens.at[j, sample]),
            (dpv.at[j], dpres.at[j, sample]),
        )
        return [
            pltpu.make_async_copy(source, target, sems.at[base + group * slots + j])
            for group, (source, target) in enumerate(pairs)
        ]

    mgv[...] = jnp.zeros_like(mgv)

    @pl.loop(0, count)
    def _(i):
        j = count - 1 - i
        for load in loads(j):
            load.wait()
        grad = acc[...]
        grad_b = grad.astype(BF16)
        ov[j] = grad_b
        for start in range(0, hidden_width, CHUNK):
            cols = slice(start, start + CHUNK)
            grad_hidden = jnp.dot(grad_b, downv[j, :, cols], preferred_element_type=F32)
            pre = prev[j, :, cols].astype(F32)
            gate = sigmoid(pre)
            hidden = pre * gate
            hidv[j, :, cols] = hidden.astype(BF16)
            dpv[j, :, cols] = (grad_hidden * (gate + hidden * (1.0 - gate))).astype(BF16)
        total = nt_dot(dpv[j], upv[j])
        state = statev[j]
        scaling = 1.0 + modv[pl.ds(j, 1), :width]
        offset = modv[pl.ds(j, 1), width:]
        inverse = lax.rsqrt(jnp.mean(state * state, axis=-1, keepdims=True) + EPSILON)
        unit = state * inverse
        nv[j] = (unit * scaling + offset).astype(BF16)
        grad_norm = total.astype(BF16).astype(F32)
        scaled = grad_norm * unit
        mgv[pl.ds(j, 1), :width] = jnp.sum(scaled, axis=0, keepdims=True)
        mgv[pl.ds(j, 1), width:] = jnp.sum(grad_norm, axis=0, keepdims=True)
        inner = jnp.mean(scaled * scaling, axis=-1, keepdims=True)
        acc[...] = grad + inverse * (grad_norm * scaling - unit * inner)
        for save in saves(j):
            save.start()

    first = acc[...].astype(BF16)
    fv[...] = first
    save_mods = pltpu.make_async_copy(mgv, mod_grads.at[sample], sems.at[base + 4 * slots])
    save_first = pltpu.make_async_copy(fv, firsts.at[sample], sems.at[base + 4 * slots + 1])
    save_mods.start()
    save_first.start()

    def finish():
        @pl.loop(0, count)
        def _(j):
            for save in saves(j):
                save.wait()

        save_first.wait()
        save_mods.wait()

    return first, finish


def forward_kernel(
    tick, has_saved, has_skip, has_kept, samples, slots, sections, width, *refs
):
    refs = list(refs)
    scal, mod, latents, incoming, up, down, skip_weight = refs[:7]
    del refs[:7]
    skip_in = refs.pop(0) if has_skip else None
    cotangent = refs.pop(0) if has_skip else None
    if has_saved:
        del refs[:3]
    if has_kept:
        del refs[:6]
    out, states, pres, skips = refs[:4]
    del refs[:4]
    if has_skip:
        out_skip, *targets = refs[:7]
        del refs[:7]
    sems = refs.pop()
    xv, sv, modv, upv, downv, skwv, statev, prev, acc, hidv = refs[:10]
    spare = refs[10:]
    stage, count = scal[0], scal[1]
    sample = tick - 2 * stage
    hidden_width = upv.shape[2]
    half = sections // 2

    @pl.when((sample >= 0) & (sample < samples))
    def _():
        copy_latents = pltpu.make_async_copy(latents.at[sample], xv, sems.at[0])
        copy_incoming = pltpu.make_async_copy(incoming, xv, sems.at[0])
        copy_mod = pltpu.make_async_copy(mod.at[sample], modv, sems.at[1])
        copy_skw = pltpu.make_async_copy(skip_weight, skwv, sems.at[2])

        def copy_up(j):
            return pltpu.make_async_copy(up.at[j], upv.at[j], sems.at[4 + j])

        def copy_down(j):
            return pltpu.make_async_copy(down.at[j], downv.at[j], sems.at[4 + slots + j])

        def save_state(j):
            return pltpu.make_async_copy(
                statev.at[j], states.at[sample, j], sems.at[4 + 2 * slots + j]
            )

        def save_pre(j):
            return pltpu.make_async_copy(prev.at[j], pres.at[sample, j], sems.at[4 + 3 * slots + j])

        save_skip = pltpu.make_async_copy(sv, skips.at[sample], sems.at[3])

        @pl.when(stage == 0)
        def _():
            copy_latents.start()

        @pl.when(stage != 0)
        def _():
            copy_incoming.start()

        copy_mod.start()
        decoder = stage >= half
        if has_skip:
            base = 4 + 4 * slots
            copy_cot = pltpu.make_async_copy(
                cotangent.at[sample], spare[0], sems.at[base + 4 * slots + 2]
            )

            @pl.when(stage == sections - 1)
            def _():
                copy_cot.start()

        @pl.when(decoder)
        def _():
            copy_skw.start()

        @pl.loop(0, count)
        def _(j):
            copy_up(j).start()
            copy_down(j).start()

        copy_incoming.wait()
        acc[...] = xv[...].astype(F32)

        @pl.when(decoder)
        def _():
            if has_skip:
                copy_skip = pltpu.make_async_copy(skip_in, sv, sems.at[3])

                @pl.when(stage == sections - 1)
                def _():
                    copy_skip.start()
                    copy_skip.wait()

                @pl.when(stage != sections - 1)
                def _():
                    sv[...] = xv[...]

            else:
                sv[...] = xv[...]
            save_skip.start()
            copy_skw.wait()
            acc[...] += jnp.dot(sv[...], skwv[...], preferred_element_type=F32)

        copy_mod.wait()

        @pl.loop(0, count)
        def _(j):
            copy_up(j).wait()
            copy_down(j).wait()
            state = acc[...]
            statev[j] = state
            scaling = modv[pl.ds(j, 1), :width]
            offset = modv[pl.ds(j, 1), width:]
            inverse = lax.rsqrt(jnp.mean(state * state, axis=-1, keepdims=True) + EPSILON)
            normed = (state * inverse * (1.0 + scaling) + offset).astype(BF16)
            for start in range(0, hidden_width, CHUNK):
                cols = slice(start, start + CHUNK)
                pre = jnp.dot(normed, upv[j, :, cols], preferred_element_type=F32)
                prev[j, :, cols] = pre.astype(BF16)
                hidv[:, cols] = (pre * sigmoid(pre)).astype(BF16)
            acc[...] = state + nt_dot(hidv[...], downv[j])
            if has_skip:

                @pl.when(stage != sections - 1)
                def _():
                    save_state(j).start()
                    save_pre(j).start()

            else:
                save_state(j).start()
                save_pre(j).start()

        def hand_on():
            xv[...] = acc[...].astype(BF16)
            save_out.start()

            @pl.loop(0, count)
            def _(j):
                save_state(j).wait()
                save_pre(j).wait()

        def turn_back():
            cv, gsv, *layers = spare
            copy_cot.wait()
            acc[...] = cv[...].astype(F32)
            first, finish = backward_layers(
                count,
                sample,
                slots,
                width,
                (modv, upv, downv, statev, prev, acc, *layers),
                targets,
                sems,
                base,
                lambda j: (),
            )
            xv[...] = first
            save_out.start()
            gsv[...] = nt_dot(first, skwv[...]).astype(BF16)
            save_grad = pltpu.make_async_copy(gsv, out_skip, sems.at[base + 4 * slots + 2])
            save_grad.start()
            finish()
            save_grad.wait()

        save_out = pltpu.make_async_copy(xv, out, sems.at[0])
        if has_skip:
            pl.when(stage == sections - 1)(turn_back)
            pl.when(stage != sections - 1)(hand_on)
        else:
            hand_on()

        @pl.when(decoder)
        def _():
            save_skip.wait()

        save_out.wait()


def forward_call(
    tick, scal, mod, latents, incoming, up, down, skip_weight, skip_in, cotangent, saved, kept
):
    samples, rows, width = latents.shape
    slots, _, hidden_width = up.shape
    shapes = (
        jax.ShapeDtypeStruct((rows, width), BF16),
        jax.ShapeDtypeStruct((samples, slots, rows, width), F32),
        jax.ShapeDtypeStruct((samples, slots, rows, hidden_width), BF16),
        jax.ShapeDtypeStruct((samples, rows, width), BF16),
    )
    scratch = []
    if skip_in is not None:
        shapes += (jax.ShapeDtypeStruct((rows, width), BF16),)
        shapes += kept_shapes(samples, slots, rows, width, hidden_width)
        scratch = [pltpu.VMEM((rows, width), BF16)] * 2
        scratch += layer_scratch(slots, rows, width, hidden_width)
    operands = [scal, mod, latents, incoming, up, down, skip_weight]
    if skip_in is not None:
        operands += [skip_in, cotangent]
    aliases = {}
    if saved is not None:
        aliases = {len(operands) + i: 1 + i for i in range(3)}
        operands += list(saved)
    if kept is not None:
        aliases |= {len(operands) + i: 5 + i for i in range(6)}
        operands += list(kept)
    out = pl.pallas_call(
        functools.partial(
            forward_kernel,
            tick,
            saved is not None,
            skip_in is not None,
            kept is not None,
            samples,
            slots,
            4,
            width,
        ),
        out_shape=shapes,
        in_specs=[SMEM] + [ANY] * (len(operands) - 1),
        out_specs=(ANY,) * len(shapes),
        input_output_aliases=aliases,
        scratch_shapes=[
            pltpu.VMEM((rows, width), BF16),
            pltpu.VMEM((rows, width), BF16),
            pltpu.VMEM((slots, 2 * width), F32),
            pltpu.VMEM((slots, width, hidden_width), BF16),
            pltpu.VMEM((slots, width, hidden_width), BF16),
            pltpu.VMEM((width, width), BF16),
            pltpu.VMEM((slots, rows, width), F32),
            pltpu.VMEM((slots, rows, hidden_width), BF16),
            pltpu.VMEM((rows, width), F32),
            pltpu.VMEM((rows, hidden_width), BF16),
            *scratch,
            pltpu.SemaphoreType.DMA((7 + 8 * slots,)),
        ],
        compiler_params=pltpu.CompilerParams(vmem_limit_bytes=SECTION_VMEM),
        cost_estimate=pl.CostEstimate(
            flops=slots * rows * width * hidden_width * 4,
            bytes_accessed=8_000_000,
            transcendentals=0,
        ),
        name=f"section_forward_{tick}",
    )(*operands)
    return out[0], out[1:4], out[4:5], out[5:]


def kept_shapes(samples, slots, rows, width, hidden_width):
    narrow = jax.ShapeDtypeStruct((slots, samples, rows, width), BF16)
    wide = jax.ShapeDtypeStruct((slots, samples, rows, hidden_width), BF16)
    return (
        narrow,
        narrow,
        wide,
        wide,
        jax.ShapeDtypeStruct((samples, slots, 2 * width), F32),
        jax.ShapeDtypeStruct((samples, rows, width), BF16),
    )


def layer_scratch(slots, rows, width, hidden_width):
    return [
        pltpu.VMEM((slots, rows, width), BF16),
        pltpu.VMEM((slots, rows, width), BF16),
        pltpu.VMEM((slots, rows, hidden_width), BF16),
        pltpu.VMEM((slots, rows, hidden_width), BF16),
        pltpu.VMEM((slots, 2 * width), F32),
        pltpu.VMEM((rows, width), BF16),
    ]


def backward_kernel(tick, has_top, has_skip, samples, slots, sections, width, *refs):
    refs = list(refs)
    scal, mod, incoming, up, down, skip_weight, states, pres = refs[:8]
    del refs[:8]
    top = refs.pop(0) if has_top else None
    skip_grad = refs.pop(0) if has_skip else None
    del refs[:6]
    out, *targets = refs[:7]
    gv, hv, modv, upv, downv, skwv, statev, prev, acc, *layers, sems = refs[7:]
    stage, count = scal[0], scal[1]
    sample = tick - 2 * (sections - 1 - stage)
    half = sections // 2

    @pl.when((sample >= 0) & (sample < samples) & (stage != sections - 1))
    def _():
        copy_incoming = pltpu.make_async_copy(incoming, gv, sems.at[0])
        copy_mod = pltpu.make_async_copy(mod.at[sample], modv, sems.at[1])
        copy_skw = pltpu.make_async_copy(skip_weight, skwv, sems.at[2])

        def copy(group, j, source, target):
            return pltpu.make_async_copy(source, target, sems.at[4 + group * slots + j])

        def loads(j):
            return (
                copy(0, j, down.at[j], downv.at[j]),
                copy(1, j, pres.at[sample, j], prev.at[j]),
                copy(2, j, up.at[j], upv.at[j]),
                copy(3, j, states.at[sample, j], statev.at[j]),
            )

        if has_top:
            copy_top = pltpu.make_async_copy(top, gv, sems.at[0])

            @pl.when(stage == sections - 2)
            def _():
                copy_top.start()

            @pl.when(stage != sections - 2)
            def _():
                copy_incoming.start()

        else:
            copy_incoming.start()
        if has_skip:
            copy_skip = pltpu.make_async_copy(skip_grad, hv, sems.at[3])

            @pl.when(stage == 0)
            def _():
                copy_skip.start()

        copy_mod.start()
        decoder = stage >= half

        @pl.loop(0, count)
        def _(i):
            for load in loads(count - 1 - i):
                load.start()

        @pl.when(decoder)
        def _():
            copy_skw.start()

        copy_incoming.wait()
        if has_skip:

            @pl.when(stage == 0)
            def _():
                copy_skip.wait()
                acc[...] = (gv[...] + hv[...]).astype(F32)

            @pl.when(stage != 0)
            def _():
                acc[...] = gv[...].astype(F32)

        else:
            acc[...] = gv[...].astype(F32)
        copy_mod.wait()
        first, finish = backward_layers(
            count,
            sample,
            slots,
            width,
            (modv, upv, downv, statev, prev, acc, *layers),
            targets,
            sems,
            4 + 4 * slots,
            loads,
        )
        gv[...] = first

        @pl.when(decoder)
        def _():
            copy_skw.wait()
            gv[...] = first + nt_dot(first, skwv[...]).astype(BF16)

        save_down = pltpu.make_async_copy(gv, out, sems.at[0])
        save_down.start()
        finish()
        save_down.wait()


def backward_call(tick, scal, mod, incoming, up, down, skip_weight, saved, top, skip_grad, kept):
    states, pres, _ = saved
    samples, slots, rows, width = states.shape
    hidden_width = up.shape[2]
    narrow = (rows, width)
    wide = (rows, hidden_width)
    shapes = (jax.ShapeDtypeStruct(narrow, BF16),)
    shapes += kept_shapes(samples, slots, rows, width, hidden_width)
    operands = [scal, mod, incoming, up, down, skip_weight, states, pres]
    if top is not None:
        operands.append(top)
    if skip_grad is not None:
        operands.append(skip_grad)
    aliases = {len(operands) + i: 1 + i for i in range(6)}
    operands += list(kept)
    out = pl.pallas_call(
        functools.partial(
            backward_kernel,
            tick,
            top is not None,
            skip_grad is not None,
            samples,
            slots,
            4,
            width,
        ),
        out_shape=shapes,
        in_specs=[SMEM] + [ANY] * (len(operands) - 1),
        out_specs=(ANY,) * len(shapes),
        input_output_aliases=aliases,
        scratch_shapes=[
            pltpu.VMEM(narrow, BF16),
            pltpu.VMEM(narrow, BF16),
            pltpu.VMEM((slots, 2 * width), F32),
            pltpu.VMEM((slots, width, hidden_width), BF16),
            pltpu.VMEM((slots, width, hidden_width), BF16),
            pltpu.VMEM((width, width), BF16),
            pltpu.VMEM((slots, *narrow), F32),
            pltpu.VMEM((slots, *wide), BF16),
            pltpu.VMEM(narrow, F32),
            *layer_scratch(slots, rows, width, hidden_width),
            pltpu.SemaphoreType.DMA((6 + 8 * slots,)),
        ],
        compiler_params=pltpu.CompilerParams(vmem_limit_bytes=SECTION_VMEM),
        cost_estimate=pl.CostEstimate(
            flops=slots * rows * width * hidden_width * 4,
            bytes_accessed=14_000_000,
            transcendentals=0,
        ),
        name=f"section_backward_{tick}",
    )(*operands)
    return out[0], out[1:]


def time_product(condition, order, mod_grads, slot):
    placed = jnp.dot(condition[...], order[...], preferred_element_type=F32)
    samples, _, lanes = mod_grads.shape
    grads = [mod_grads[sample, slot : slot + 1, :] for sample in range(samples)]
    grads.append(jnp.zeros((condition.shape[0] - samples, lanes), F32))
    return lax.dot_general(
        placed, jnp.concatenate(grads, axis=0), TN, preferred_element_type=F32
    )


def up_grad_kernel(
    scal, norms, dpres, order, condition, mod_grads, mine, theirs, nv, dv, product, packed, sems
):
    count, core = scal[1], scal[2]
    slots = nv.shape[0]
    block, lanes = mine.shape[2:]

    def loads(j):
        return (
            pltpu.make_async_copy(norms.at[j], nv.at[j], sems.at[0, j]),
            pltpu.make_async_copy(dpres.at[j], dv.at[j], sems.at[1, j]),
        )

    def saves(j):
        place = pl.ds(2 * j, 2)
        return (
            pltpu.make_async_copy(packed.at[1, j], theirs.at[:, place], sems.at[2, j]),
            pltpu.make_async_copy(packed.at[0, j], mine.at[:, place], sems.at[3, j]),
        )

    def pack(j):
        for target, side in ((1, 1 - core), (0, core)):
            for i in range(4):
                for half in range(2):
                    low = pl.multiple_of((side * 4 + i) * block, 8)
                    cols = slice(half * lanes, (half + 1) * lanes)
                    packed[target, j, i, half] = product[pl.ds(low, block), cols].astype(BF16)

    @pl.loop(0, count)
    def _(j):
        for load in loads(j):
            load.start()

    for half in range(2):
        product[:, half * lanes : (half + 1) * lanes] = time_product(
            condition, order, mod_grads, half
        )

    pack(slots)
    for save in saves(slots):
        save.start()

    @pl.loop(0, slots)
    def _(j):
        @pl.when(j < count)
        def _():
            for load in loads(j):
                load.wait()
            placed = jnp.dot(nv[j], order[...], preferred_element_type=F32).astype(BF16)
            product[...] = jnp.dot(placed.T, dv[j], preferred_element_type=F32)
            pack(j)

        @pl.when(j >= count)
        def _():
            for target in range(2):
                packed[target, j] = jnp.zeros(packed.shape[2:], BF16)

        for save in saves(j):
            save.start()

    @pl.loop(0, slots + 1)
    def _(j):
        for save in saves(j):
            save.wait()


def up_grad_call(scal, norms, dpres, order, condition, mod_grads):
    slots, rows, width = norms.shape
    hidden_width = dpres.shape[2]
    block = width // 8
    shape = jax.ShapeDtypeStruct((4, 2 * slots + 2, block, hidden_width // 2), BF16)
    return pl.pallas_call(
        up_grad_kernel,
        out_shape=(shape, shape),
        in_specs=[SMEM, ANY, ANY, VMEM, VMEM, VMEM],
        out_specs=(ANY, ANY),
        scratch_shapes=[
            pltpu.VMEM((slots, rows, width), BF16),
            pltpu.VMEM((slots, rows, hidden_width), BF16),
            pltpu.VMEM((width, hidden_width), F32),
            pltpu.VMEM((2, slots + 1, 4, 2, block, hidden_width // 2), BF16),
            pltpu.SemaphoreType.DMA((4, slots + 1)),
        ],
        compiler_params=pltpu.CompilerParams(vmem_limit_bytes=GRAD_VMEM),
        cost_estimate=pl.CostEstimate(
            flops=2 * slots * rows * width * hidden_width,
            bytes_accessed=12_000_000,
            transcendentals=0,
        ),
        name="up_grad",
    )(scal, norms, dpres, order, condition, mod_grads)


def down_grad_kernel(
    scal,
    hiddens,
    outs,
    skips,
    firsts,
    order,
    condition,
    mod_grads,
    mine,
    theirs,
    hv,
    gv,
    sv,
    fv,
    product,
    prod_time,
    prod_skip,
    packed,
    sems,
):
    stage, count, core = scal[0], scal[1], scal[2]
    slots = hv.shape[0]
    block, lanes = mine.shape[2:]
    width = lanes // 2
    load_skip = pltpu.make_async_copy(skips, sv, sems.at[0, slots])
    load_first = pltpu.make_async_copy(firsts, fv, sems.at[1, slots])

    def loads(j):
        return (
            pltpu.make_async_copy(hiddens.at[j], hv.at[j], sems.at[0, j]),
            pltpu.make_async_copy(outs.at[j], gv.at[j], sems.at[1, j]),
        )

    def saves(j):
        place = pl.ds(2 * j, 2)
        return (
            pltpu.make_async_copy(packed.at[1, j], theirs.at[:, place], sems.at[2, j]),
            pltpu.make_async_copy(packed.at[0, j], mine.at[:, place], sems.at[3, j]),
        )

    @pl.when(stage >= 2)
    def _():
        load_skip.start()
        load_first.start()

    @pl.loop(0, count)
    def _(j):
        for load in loads(j):
            load.start()

    prod_time[...] = time_product(condition, order, mod_grads, slots - 1)
    prod_skip[...] = jnp.zeros_like(prod_skip)

    @pl.when(stage >= 2)
    def _():
        load_skip.wait()
        load_first.wait()
        placed = jnp.dot(sv[...], order[...], preferred_element_type=F32).astype(BF16)
        prod_skip[:, :width] = lax.dot_general(placed, fv[...], TN, preferred_element_type=F32)

    for target, side in ((1, 1 - core), (0, core)):
        for y in range(4):
            low = pl.multiple_of((side * 4 + y) * block, 8)
            packed[target, slots, y, 0] = prod_time[pl.ds(low, block), :].astype(BF16)
            packed[target, slots, y, 1] = prod_skip[pl.ds(low, block), :].astype(BF16)
    for save in saves(slots):
        save.start()

    @pl.loop(0, slots)
    def _(j):
        @pl.when(j < count)
        def _():
            for load in loads(j):
                load.wait()
            for start in range(0, hv.shape[2], CHUNK):
                cols = slice(start, start + CHUNK)
                product[cols, :] = lax.dot_general(
                    hv[j, :, cols], gv[j], TN, preferred_element_type=F32
                )
            for target, side in ((1, 1 - core), (0, core)):
                for y in range(4):
                    for pair in range(2):
                        low = pl.multiple_of((8 * y + 4 * pair + side) * block, 8)
                        high = pl.multiple_of((8 * y + 4 * pair + 2 + side) * block, 8)
                        packed[target, j, y, pair] = jnp.concatenate(
                            [product[pl.ds(low, block), :], product[pl.ds(high, block), :]],
                            axis=1,
                        ).astype(BF16)

        @pl.when(j >= count)
        def _():
            for target in range(2):
                packed[target, j] = jnp.zeros(packed.shape[2:], BF16)

        for save in saves(j):
            save.start()

    @pl.loop(0, slots + 1)
    def _(j):
        for save in saves(j):
            save.wait()


def down_grad_call(scal, hiddens, outs, skips, firsts, order, condition, mod_grads):
    slots, rows, hidden_width = hiddens.shape
    width = outs.shape[2]
    block = width // 8
    shape = jax.ShapeDtypeStruct((4, 2 * slots + 2, block, 2 * width), BF16)
    return pl.pallas_call(
        down_grad_kernel,
        out_shape=(shape, shape),
        in_specs=[SMEM, ANY, ANY, ANY, ANY, VMEM, VMEM, VMEM],
        out_specs=(ANY, ANY),
        scratch_shapes=[
            pltpu.VMEM((slots, rows, hidden_width), BF16),
            pltpu.VMEM((slots, rows, width), BF16),
            pltpu.VMEM((rows, width), BF16),
            pltpu.VMEM((rows, width), BF16),
            pltpu.VMEM((hidden_width, width), F32),
            pltpu.VMEM((width, 2 * width), F32),
            pltpu.VMEM((width, 2 * width), F32),
            pltpu.VMEM((2, slots + 1, 4, 2, block, 2 * width), BF16),
            pltpu.SemaphoreType.DMA((4, slots + 1)),
        ],
        compiler_params=pltpu.CompilerParams(vmem_limit_bytes=GRAD_VMEM),
        cost_estimate=pl.CostEstimate(
            flops=2 * slots * rows * width * hidden_width,
            bytes_accessed=12_000_000,
            transcendentals=0,
        ),
        name="down_grad",
    )(scal, hiddens, outs, skips, firsts, order, condition, mod_grads)


def block_order(width, first, second):
    block = width // 32
    matrix = np.zeros((width, width), ml_dtypes.bfloat16)
    for y in range(4):
        for x in range(4):
            for core in range(2):
                where = {"x": x, "y": y}
                place = (core * 4 + where[first]) * 4 + where[second]
                source = 8 * y + 2 * x + core
                for r in range(block):
                    matrix[source * block + r, place * block + r] = 1
    return jnp.asarray(matrix)


def shifted(size, distance):
    return [(i, (i + distance) % size) for i in range(size)]


def paired(pieces, axis):
    index = lax.axis_index(axis)
    other = 3 - index
    sent = jnp.stack([pieces(index ^ 1), pieces(other ^ 1)])
    arrived = lax.ppermute(sent, axis, [(i, i ^ 1) for i in range(4)])
    passed = add(pieces(other), arrived[1])
    last = lax.ppermute(passed, axis, [(i, 3 - i) for i in range(4)])
    return pieces(index).astype(F32) + arrived[0].astype(F32) + last.astype(F32)


def halved(pieces, axis):
    size = lax.axis_size(axis)
    index = lax.axis_index(axis)
    own, ahead, across, behind = (pieces(lax.rem(index + d, size)) for d in (0, 1, 2, 3))
    cut = own.shape[0] // 2
    forward, backward = shifted(size, 1), shifted(size, size - 1)
    from_behind = lax.ppermute(jnp.concatenate([across[:cut], ahead[cut:]]), axis, forward)
    from_ahead = lax.ppermute(jnp.concatenate([across[cut:], behind[:cut]]), axis, backward)
    rest = own.shape[0] - cut
    passed_on = lax.ppermute(add(ahead[:cut], from_behind[:cut]), axis, forward)
    passed_back = lax.ppermute(add(behind[cut:], from_ahead[:rest]), axis, backward)
    low = add(own[:cut], from_ahead[rest:], passed_on)
    high = add(own[cut:], from_behind[cut:], passed_back)
    return jnp.concatenate([low, high])


def add(*terms):
    total = terms[0].astype(F32)
    for term in terms[1:]:
        total = total + term.astype(F32)
    return total.astype(BF16)


def take(value, index, dim):
    return lax.dynamic_index_in_dim(value, index, dim, keepdims=False)


def per_device(
    latents, cotangent, timesteps, layer_count, up_weight, down_weight, time_weight, skip_weight
):
    sections = lax.axis_size("pipe")
    stage = lax.axis_index("pipe")
    core = lax.axis_index("core")
    samples, rows, width = latents.shape
    up, down, skip_mat = up_weight[0], down_weight[0].swapaxes(1, 2), skip_weight[0]
    slots, _, hidden_width = up.shape
    scal = jnp.stack([stage, layer_count[0], core, core]).astype(jnp.int32)
    condition = jax.nn.silu(embedding(timesteps, width // 2)).astype(BF16)
    modulation = jnp.einsum("mt,jtc->mjc", condition, time_weight[0], preferred_element_type=F32)
    order_x = block_order(width, "x", "y")
    order_y = block_order(width, "y", "x")

    padded = jnp.concatenate([condition, jnp.zeros((16 - samples, width), BF16)])

    lead = 2 * (sections - 1)
    ticks = samples + lead
    empty = jnp.zeros((rows, width), BF16)
    moved, skips_moved, tops, skip_grads = {}, {}, {}, {}
    saved, kept = None, None
    for tick in range(ticks):
        sent, saved, sent_skip, made = forward_call(
            tick,
            scal,
            modulation,
            latents,
            moved.get(tick - 2, empty),
            up,
            down,
            skip_mat,
            skips_moved.get(tick - lead),
            cotangent,
            saved,
            kept,
        )
        pairs = [(z, z + 1) for z in range(sections - 1) if 0 <= tick - 2 * z < samples]
        if pairs:
            moved[tick] = lax.ppermute(sent, "pipe", pairs)
        if tick < samples:
            skips_moved[tick] = lax.ppermute(sent, "pipe", [(0, sections - 1)])
        if tick >= lead:
            kept = made
            tops[tick - lead] = lax.ppermute(sent, "pipe", [(sections - 1, sections - 2)])
            skip_grads[tick - lead] = lax.ppermute(sent_skip[0], "pipe", [(sections - 1, 0)])
    skips = saved[2]

    moved = {}
    for tick in range(2, ticks):
        incoming, top = moved.get(tick - 2), tops.get(tick - 2)
        if incoming is None:
            incoming, top = top, None
        sent, kept = backward_call(
            tick,
            scal,
            modulation,
            incoming,
            up,
            down,
            skip_mat,
            saved,
            top,
            skip_grads.get(tick - lead),
            kept,
        )
        pairs = [
            (z, z - 1)
            for z in range(1, sections - 1)
            if 0 <= tick - 2 * (sections - 1 - z) < samples
        ]
        if pairs:
            moved[tick] = lax.ppermute(sent, "pipe", pairs)
    norms, outs, hiddens, dpres, mod_grads, firsts = kept
    total_rows = samples * rows

    mine_up, theirs_up = up_grad_call(
        scal,
        norms.reshape(slots, total_rows, width),
        dpres.reshape(slots, total_rows, hidden_width),
        order_x,
        padded,
        mod_grads,
    )
    other_up = lax.ppermute(theirs_up, "core", [(0, 1), (1, 0)])
    mine_down, theirs_down = down_grad_call(
        scal,
        hiddens.reshape(slots, total_rows, hidden_width),
        outs.reshape(slots, total_rows, width),
        skips.reshape(total_rows, width),
        firsts.reshape(total_rows, width),
        order_y,
        padded,
        mod_grads,
    )
    other_down = lax.ppermute(theirs_down, "core", [(0, 1), (1, 0)])

    sum_up = halved(lambda i: add(take(mine_up, i, 0), take(other_up, i, 0)), "x")
    sum_down = halved(lambda i: add(take(mine_down, i, 0), take(other_down, i, 0)), "y")
    block, part = width // 8, width // 32
    blocks = 2 * slots
    down_part = sum_down[:blocks].reshape(slots, 2, block, 2, width).transpose(1, 3, 0, 2, 4)
    down_part = down_part.reshape(4, slots * block, width)
    time_part = sum_down[blocks].reshape(4, part, 2, width).transpose(0, 2, 1, 3)
    skip_part = sum_down[blocks + 1, :, :width].reshape(4, part, width)
    down_part = jnp.concatenate(
        [down_part, time_part.reshape(4, 2 * part, width), skip_part], axis=1
    )
    up_part = sum_up.reshape(blocks + 2, 4, part, 2 * width)

    final_up = paired(lambda i: take(up_part, i, 1), "y")
    final_down = paired(lambda i: take(down_part, i, 0), "x")
    grad_up = final_up[:blocks].reshape(slots, 2, part, 2 * width).transpose(0, 2, 1, 3)
    grad_up = grad_up.reshape(slots, part, hidden_width)
    grad_down = final_down[: slots * block].reshape(slots, block, width)
    last_time = final_down[slots * block : slots * block + 2 * part].reshape(2, part, width)
    last_time = last_time.transpose(1, 0, 2).reshape(1, part, 2 * width)
    grad_time = jnp.concatenate([final_up[blocks:], last_time])
    grad_skip = final_down[slots * block + 2 * part :]
    return (grad_up[None], grad_down[None], grad_time[None], grad_skip[None])


def solution(mesh):
    split = Mesh(
        mesh.devices.reshape(4, 4, 2, mesh.devices.shape[1]), ("y", "x", "core", "pipe")
    )
    dp = ("y", "x", "core")
    placed = (
        P(dp, None, None),
        P(dp, None, None),
        P(dp),
        P("pipe"),
        P("pipe", None, None, None),
        P("pipe", None, None, None),
        P("pipe", None, None, None),
        P("pipe", None, None),
    )
    return jax.shard_map(
        per_device,
        mesh=split,
        in_specs=placed,
        out_specs=(
            P("pipe", None, dp, None),
            P("pipe", None, dp, None),
            P("pipe", None, dp, None),
            P("pipe", dp, None),
        ),
        check_vma=False,
    )
```

time: 173 us -> 164 us (0.948); the launches traced: 172 us -> 165 us
  waiting for transfers between devices: 52.5 us -> 44.5 us
  Pallas kernels: 54 us -> 60.7 us
  starting transfers between devices: 47.9 us -> 44 us
    ppermute x9 -> x10, waiting for transfers between devices: 33 us -> 27.8 us  [the longest x3 23.8 us: per_device(): lax.ppermute(sent_skip[0], 'pipe', [(sections - 1, 0)])]
    pallas_call x9, Pallas kernels: 17.6 us -> 21.6 us  [forward_call(): pl.pallas_call(functools.partial(forward_kernel, tick, saved is not None,...]
    ppermute x14 -> x12, waiting for transfers between devices: 10.3 us -> 6.72 us  [per_device(): moved[tick] = lax.ppermute(sent, 'pipe', pairs)]
    pallas_call x11 -> x9, Pallas kernels: 36.4 us -> 39.1 us  [the longest x7 23.4 us: backward_call(): pl.pallas_call(functools.partial(backward_kernel, tick, top is not None,...]
    ppermute x9 -> x10, starting transfers between devices: 16.2 us -> 13.7 us  [the longest x2 5.92 us: paired(): last = lax.ppermute(passed, axis, [(i, 3 - i) for i in range(4)])]
    ppermute x14 -> x12, starting transfers between devices: 14 us -> 11.8 us  [per_device(): moved[tick] = lax.ppermute(sent, 'pipe', pairs)]
    ppermute x2, waiting for transfers between devices: 2.49 us -> 4.72 us  [halved(): passed_on = lax.ppermute(add(ahead[:cut], from_behind[:cut]), axis, forward)]
    convert_element_type x8 -> x10, other arithmetic: 5.77 us -> 5.78 us  [add(): return total.astype(BF16)]
  transfers between devices with their start and end apart: 36 -> 35, of which waited for: 10 -> 10; matrix products, arithmetic and copies ran while one was open for 6% -> 6% of each run, Pallas kernels for 21% -> 25%
where the time goes in v1:
time: 164 us; the launch traced here: 165 us
  Pallas kernels  60.7 us (37%)
  waiting for transfers between devices  44.5 us (27%)
  starting transfers between devices  44 us (27%)
  other arithmetic  7.28 us (4%)
  local copies, waits for them, and re-layouts  6.19 us (4%)
  between operations  2.24 us (1%)
    ppermute x3, waiting for transfers between devices, per_device(): lax.ppermute(sent_skip[0], 'pipe', [(sections - 1, 0)])  23.8 us
    pallas_call x7, Pallas kernels, backward_call(): pl.pallas_call(functools.partial(backward_kernel, tick, top is not None,...  23.4 us
    pallas_call x9, Pallas kernels, forward_call(): pl.pallas_call(functools.partial(forward_kernel, tick, saved is not None,...  21.6 us
    ppermute x12, starting transfers between devices, per_device(): moved[tick] = lax.ppermute(sent, 'pipe', pairs)  11.8 us
    pallas_call x1, Pallas kernels, up_grad_call(): pl.pallas_call(up_grad_kernel, out_shape=(shape, shape), in_specs=[SMEM,...  8.09 us
    pallas_call x1, Pallas kernels, down_grad_call(): pl.pallas_call(down_grad_kernel, out_shape=(shape, shape), in_specs=[SMEM...  7.64 us
    ppermute x2, starting transfers between devices, halved(): lax.ppermute(jnp.concatenate([across[cut:], behind[:cut]]), axis, backward)  6.92 us
    ppermute x2, starting transfers between devices, halved(): lax.ppermute(add(behind[cut:], from_ahead[:rest]), axis, backward)  6.81 us
  transfers between devices with their start and end apart: 35, of which 10 were waited for; matrix products, arithmetic and copies ran while one was open for 6% of the time, Pallas kernels for 25%

profile of v1, /device:TPU:0, one launch (start us, length us, event | category | flops | bytes accessed | tf_op | source)
XLA Modules:
  0.0 165.2 jit_solution(17573685770935168861)
XLA Ops:
  2.7 0.9 copy-done.1
  3.6 5.5 %section_forward_0.1 = (bf16[192,320]{1,0:T(8,128)(2,1)S(1)}, f32[3,3,192,320]{3,2,1,0:T(8,128)}, bf16[3,3,192,1280]{3,2,1,0:T(8,128)(2,1)}, bf16[3,192,320]{2,1,0:T(8,128)(2,1)}) custom-call(s32[4]{0:T(128)S(1)} %pad_add_fusion.refs_0_.scal, f32[3,3,640]{2,1,0:T(4,128)S(1)} %copy.129.refs_1_, bf16[3,192,320]{2,1,0:T(8,128)(2,1)} %refs_2_.17, ...), custom_call_target="tpu_custom_call" | custom-call | flops 943718400 | bytes 8000000 | tf_op jit(solution)/shard_map/section_forward_0/pallas_call | solution.py:313
  9.1 1.3 collective-permute-start
  10.4 5.5 %section_forward_1.1 = (bf16[192,320]{1,0:T(8,128)(2,1)S(1)}, f32[3,3,192,320]{3,2,1,0:T(8,128)}, bf16[3,3,192,1280]{3,2,1,0:T(8,128)(2,1)}, bf16[3,192,320]{2,1,0:T(8,128)(2,1)}) custom-call(s32[4]{0:T(128)S(1)} %pad_add_fusion.refs_0_.scal, f32[3,3,640]{2,1,0:T(4,128)S(1)} %copy.129.refs_1_, ...), custom_call_target="tpu_custom_call", output_to_operand_aliasing={{1}: (7, {}), {2}: (8, {}), {3}: (9, {})} | custom-call | flops 943718400 | bytes 8000000 | tf_op jit(solution)/shard_map/section_forward_1/pallas_call | solution.py:313
  15.9 1.3 collective-permute-start.2
  17.2 5.5 %section_forward_2.1 = (bf16[192,320]{1,0:T(8,128)(2,1)S(1)}, f32[3,3,192,320]{3,2,1,0:T(8,128)}, bf16[3,3,192,1280]{3,2,1,0:T(8,128)(2,1)}, bf16[3,192,320]{2,1,0:T(8,128)(2,1)}) custom-call(s32[4]{0:T(128)S(1)} %pad_add_fusion.refs_0_.scal, f32[3,3,640]{2,1,0:T(4,128)S(1)} %copy.129.refs_1_, ...), custom_call_target="tpu_custom_call", output_to_operand_aliasing={{1}: (7, {}), {2}: (8, {}), {3}: (9, {})} | custom-call | flops 943718400 | bytes 8000000 | tf_op jit(solution)/shard_map/section_forward_2/pallas_call | solution.py:313
  22.7 1.3 collective-permute-start.1
  24.0 0.8 section_forward_3.1
  25.6 1.3 collective-permute-start.4
  26.9 0.8 section_forward_4.1
  28.4 1.3 collective-permute-start.10
  31.2 1.3 collective-permute-start.8
  32.6 0.8 section_forward_6.1
  34.8 0.8 section_forward_7.1
  36.3 1.0 section_forward_8.1
  37.4 0.8 section_backward_2.1
  39.6 1.3 collective-permute-start.15
  40.9 0.8 section_backward_3.1
  42.4 0.8 section_backward_4.1
  43.3 1.3 collective-permute-start.14
  44.6 1.3 collective-permute-start.20
  45.9 1.3 collective-permute-start.18
  47.2 0.8 section_backward_5.1
  48.0 1.3 collective-permute-start.19
  49.3 23.8 %collective-permute-done.15.refs_8_ = bf16[192,320]{1,0:T(8,128)(2,1)S(1)} collective-permute-done((bf16[192,320]{1,0:T(8,128)(2,1)S(1)}, bf16[192,320]{1,0:T(8,128)(2,1)S(1)}, u32[]{:S(2)}, u32[]{:S(2)}) %collective-permute-start.15) | collective-permute-done | bytes 122912 | tf_op jit(solution)/shard_map/ppermute | solution.py:871
  73.1 5.1 %collective-permute-done.14.refs_2_ = bf16[192,320]{1,0:T(8,128)(2,1)S(1)} collective-permute-done((bf16[192,320]{1,0:T(8,128)(2,1)S(1)}, bf16[192,320]{1,0:T(8,128)(2,1)S(1)}, u32[]{:S(2)}, u32[]{:S(2)}) %collective-permute-start.14) | collective-permute-done | bytes 122912 | tf_op jit(solution)/shard_map/ppermute | solution.py:898
  78.2 6.7 %section_backward_6.1 = (bf16[192,320]{1,0:T(8,128)(2,1)S(1)}, bf16[3,3,192,320]{3,2,1,0:T(8,128)(2,1)}, bf16[3,3,192,320]{3,2,1,0:T(8,128)(2,1)}, bf16[3,3,192,...) custom-call(s32[4]{0:T(128)S(1)} %pad_add_fusion.refs_0_.scal, ...), custom_call_target="tpu_custom_call", output_to_operand_aliasing={{1}: (9, {}), {2}: (10, {}), {3}: (11, {}), {4}: (12, {}), ... | custom-call | flops 943718400 | bytes 14000000 | tf_op jit(solution)/shard_map/section_backward_6/pallas_call | solution.py:494
  84.9 1.3 collective-permute-start.17
  87.3 6.7 %section_backward_7.1 = (bf16[192,320]{1,0:T(8,128)(2,1)}, bf16[3,3,192,320]{3,2,1,0:T(8,128)(2,1)}, bf16[3,3,192,320]{3,2,1,0:T(8,128)(2,1)}, bf16[3,3,192,1280...) custom-call(s32[4]{0:T(128)S(1)} %pad_add_fusion.refs_0_.scal, ...), custom_call_target="tpu_custom_call", output_to_operand_aliasing={{1}: (9, {}), {2}: (10, {}), {3}: (11, {}), {4}: (12, {}), ... | custom-call | flops 943718400 | bytes 14000000 | tf_op jit(solution)/shard_map/section_backward_7/pallas_call | solution.py:494
  94.0 1.1 collective-permute-done.17.refs_2_
  95.1 6.7 %section_backward_8.1 = (bf16[192,320]{1,0:T(8,128)(2,1)}, bf16[3,3,192,320]{3,2,1,0:T(8,128)(2,1)}, bf16[3,3,192,320]{3,2,1,0:T(8,128)(2,1)}, bf16[3,3,192,1280...) custom-call(s32[4]{0:T(128)S(1)} %pad_add_fusion.refs_0_.scal, ...), custom_call_target="tpu_custom_call", output_to_operand_aliasing={{1}: (9, {}), {2}: (10, {}), {3}: (11, {}), {4}: (12, {}), ... | custom-call | flops 943718400 | bytes 14000000 | tf_op jit(solution)/shard_map/section_backward_8/pallas_call | solution.py:494
  102.4 7.6 %down_grad.1 = (bf16[4,8,40,640]{3,2,1,0:T(8,128)(2,1)}, bf16[4,8,40,640]{3,2,1,0:T(8,128)(2,1)}) custom-call(s32[4]{0:T(128)} %copy-done.4, bf16[3,576,1280]{2,1,0:T(8,128)(2,1)} %bitcast.161, bf16[3,576,320]{2,1,0:T(8,128)(2,1)} %bitcast.164, bf16[576,320]{1,0:T(8,128)(2,1)} %bitcast.166, bf16[576,320]{1,0:T(8,128)(2,1)} %bitcast.165, ...), custom_call_target="tpu_custom_call" | custom-call | flops 1415577600 | bytes 12000000 | tf_op jit(solution)/shard_map/down_grad/pallas_call | solution.py:745
  110.1 8.1 %up_grad.1 = (bf16[4,8,40,640]{3,2,1,0:T(8,128)(2,1)}, bf16[4,8,40,640]{3,2,1,0:T(8,128)(2,1)}) custom-call(s32[4]{0:T(128)} %copy-done.4, bf16[3,576,320]{2,1,0:T(8,128)(2,1)} %bitcast.163, bf16[3,576,1280]{2,1,0:T(8,128)(2,1)} %bitcast.162, bf16[320,320]{1,0:T(8,128)(2,1)} %constant.113.clone.order, bf16[16,320]{1,0:T(8,128)(2,1)} %concatenate.31.condition, ...), custom_call_target="tpu_custom_call" | custom-call | flops 1415577600 | bytes 12000000 | tf_op jit(solution)/shard_map/up_grad/pallas_call | solution.py:614
  118.8 2.3 %add_convert_fusion.3 = (bf16[1,8,40,640]{3,2,1,0:T(8,128)(2,1)S(1)}, bf16[1,8,40,640]{3,2,1,0:T(8,128)(2,1)S(1)}, bf16[1,8,40,640]{3,2,1,0:T(8,128)(2,1)S(1)}, bf16[1,8,40,640]{3,2,1,0:T(8,128)(2,1)S(1)}) fusion(bf16[4,8,40,640]{3,2,1,0:T(8,128)(2,1)} %collective-permute-done.28, s32[]{:T(128)S(6)} %select_n.67, ...), kind=kLoop, calls=%fused_computation.5 | loop fusion | flops 3276800 | bytes 4915216 | tf_op jit(solution)/shard_map/convert_element_type | solution.py:819
  121.2 4.1 %collective-permute-start.29 = (bf16[8,40,640]{2,1,0:T(8,128)(2,1)S(1)}, bf16[8,40,640]{2,1,0:T(8,128)(2,1)S(1)}, u32[]{:S(2)}, u32[]{:S(2)}) collective-permute-start(bf16[8,40,640]{2,1,0:T(8,128)(2,1)S(1)} %pad_maximum_fusion.4), channel_id=1, source_target_pairs={{0,96},{32,0},{64,32},{96,64},{1,97},{33,1},{65,33},{97,65},{2,98}... | collective-permute-start | bytes 1228808 | tf_op jit(solution)/shard_map/ppermute | solution.py:806
  126.0 2.9 %collective-permute-start.22 = (bf16[8,40,640]{2,1,0:T(8,128)(2,1)S(1)}, bf16[8,40,640]{2,1,0:T(8,128)(2,1)S(1)}, u32[]{:S(2)}, u32[]{:S(2)}) collective-permute-start(bf16[8,40,640]{2,1,0:T(8,128)(2,1)S(1)} %pad_maximum_fusion.1), channel_id=1, source_target_pairs={{0,24},{8,0},{16,8},{24,16},{1,25},{9,1},{17,9},{25,17},{2,26},{10... | collective-permute-start | bytes 1228808 | tf_op jit(solution)/shard_map/ppermute | solution.py:806
  129.1 5.2 %collective-permute-done.29 = bf16[8,40,640]{2,1,0:T(8,128)(2,1)S(1)} collective-permute-done((bf16[8,40,640]{2,1,0:T(8,128)(2,1)S(1)}, bf16[8,40,640]{2,1,0:T(8,128)(2,1)S(1)}, u32[]{:S(2)}, u32[]{:S(2)}) %collective-permute-start.29) | collective-permute-done | bytes 409632 | tf_op jit(solution)/shard_map/ppermute | solution.py:806
  134.3 3.8 %collective-permute-start.32 = (bf16[4,40,640]{2,1,0:T(8,128)(2,1)S(1)}, bf16[4,40,640]{2,1,0:T(8,128)(2,1)S(1)}, u32[]{:S(2)}, u32[]{:S(2)}) collective-permute-start(bf16[4,40,640]{2,1,0:T(8,128)(2,1)S(1)} %fusion.2), channel_id=1, source_target_pairs={{0,96},{32,0},{64,32},{96,64},{1,97},{33,1},{65,33},{97,65},{2,98}... | collective-permute-start | bytes 614408 | tf_op jit(solution)/shard_map/ppermute | solution.py:809
  139.0 3.0 %collective-permute-start.25 = (bf16[4,40,640]{2,1,0:T(8,128)(2,1)}, bf16[4,40,640]{2,1,0:T(8,128)(2,1)S(1)}, u32[]{:S(2)}, u32[]{:S(2)}) collective-permute-start(bf16[4,40,640]{2,1,0:T(8,128)(2,1)} %fusion.8), channel_id=1, source_target_pairs={{0,24},{8,0},{16,8},{24,16},{1,25},{9,1},{17,9},{25,17},{2,26},{10... | collective-permute-start | bytes 614408 | tf_op jit(solution)/shard_map/ppermute | solution.py:809
  142.9 2.6 %collective-permute-done.31 = bf16[4,40,640]{2,1,0:T(8,128)(2,1)S(1)} collective-permute-done((bf16[4,40,640]{2,1,0:T(8,128)(2,1)S(1)}, bf16[4,40,640]{2,1,0:T(8,128)(2,1)S(1)}, u32[]{:S(2)}, u32[]{:S(2)}) %collective-permute-start.31) | collective-permute-done | bytes 204832 | tf_op jit(solution)/shard_map/ppermute | solution.py:808
  146.4 1.6 collective-permute-start.33
  148.0 2.2 %collective-permute-done.24 = bf16[4,40,640]{2,1,0:T(8,128)(2,1)} collective-permute-done((bf16[4,40,640]{2,1,0:T(8,128)(2,1)}, bf16[4,40,640]{2,1,0:T(8,128)(2,1)}, u32[]{:S(2)}, u32[]{:S(2)}) %collective-permute-start.24) | collective-permute-done | bytes 204832 | tf_op jit(solution)/shard_map/ppermute | solution.py:808
  150.1 1.2 fusion.13
  152.6 2.9 %collective-permute-start.34 = (bf16[150,320]{1,0:T(8,128)(2,1)S(1)}, bf16[150,320]{1,0:T(8,128)(2,1)S(1)}, u32[]{:S(2)}, u32[]{:S(2)}) collective-permute-start(bf16[150,320]{1,0:T(8,128)(2,1)S(1)} %fusion.16), channel_id=1, source_target_pairs={{0,24},{8,16},{16,8},{24,0},{1,25},{9,17},{17,9},{25,1},{2,26},{10... | collective-permute-start | bytes 288008 | tf_op jit(solution)/shard_map/ppermute | solution.py:795
  155.5 1.9 %collective-permute-done.26 = bf16[2,8,10,640]{3,1,2,0:T(8,128)(2,1)S(1)} collective-permute-done((bf16[2,8,10,640]{3,1,2,0:T(8,128)(2,1)S(1)}, bf16[2,8,10,640]{3,1,2,0:T(8,128)(2,1)S(1)}, u32[]{:S(2)}, u32[]{:S(2)}) %collective-permute-start.26) | collective-permute-done | bytes 204832 | tf_op jit(solution)/shard_map/ppermute | solution.py:793
  157.4 3.0 %collective-permute-start.27 = (bf16[8,10,640]{2,0,1:T(8,128)(2,1)S(1)}, bf16[8,10,640]{2,0,1:T(8,128)(2,1)S(1)}, u32[]{:S(2)}, u32[]{:S(2)}) collective-permute-start(bf16[8,10,640]{2,0,1:T(8,128)(2,1)S(1)} %fusion.14), channel_id=1, source_target_pairs={{0,96},{32,64},{64,32},{96,0},{1,97},{33,65},{65,33},{97,1},{2,98}... | collective-permute-start | bytes 307208 | tf_op jit(solution)/shard_map/ppermute | solution.py:795
  161.9 1.4 collective-permute-done.27
  164.3 0.9 broadcast_in_dim_reshape.6
  (114 shorter events, 17.8 us)
Async XLA Ops:
  0.6 1.6 copy-start
  2.7 92.4 %copy-start.4 = (s32[4]{0:T(128)}, s32[4]{0:T(128)S(1)}, u32[]{:S(2)}) copy-start(s32[4]{0:T(128)S(1)} %pad_add_fusion.refs_0_.scal) | copy-start | bytes 52
  2.7 0.9 copy-start.1
  9.1 8.1 %collective-permute-start = (bf16[192,320]{1,0:T(8,128)(2,1)S(1)}, bf16[192,320]{1,0:T(8,128)(2,1)S(1)}, u32[]{:S(2)}, u32[]{:S(2)}) collective-permute-start(bf16[192,320]{1,0:T(8,128)(2,1)S(1)} %get-tuple-element.112), channel_id=1, source_target_pairs={{0,1},{4,5},{8,9},{12,13},{16,17},{20,21},{24,25},{28,29},{32,33},... | collective-permute-start | bytes 368648 | tf_op jit(solution)/shard_map/ppermute | solution.py:865
  10.4 6.8 %copy-start.2 = (bf16[1,320,320]{2,1,0:T(8,128)(2,1)S(1)}, bf16[1,320,320]{2,1,0:T(8,128)(2,1)}, u32[]{:S(2)}) copy-start(bf16[1,320,320]{2,1,0:T(8,128)(2,1)} %param.17) | copy-start | bytes 614404
  15.9 8.1 %collective-permute-start.2 = (bf16[192,320]{1,0:T(8,128)(2,1)S(1)}, bf16[192,320]{1,0:T(8,128)(2,1)S(1)}, u32[]{:S(2)}, u32[]{:S(2)}) collective-permute-start(bf16[192,320]{1,0:T(8,128)(2,1)S(1)} %get-tuple-element.120), channel_id=1, source_target_pairs={{0,1},{4,5},{8,9},{12,13},{16,17},{20,21},{24,25},{28,29},{32,33},... | collective-permute-start | bytes 368648 | tf_op jit(solution)/shard_map/ppermute | solution.py:865
  22.7 4.1 %collective-permute-start.1 = (bf16[192,320]{1,0:T(8,128)(2,1)S(1)}, bf16[192,320]{1,0:T(8,128)(2,1)S(1)}, u32[]{:S(2)}, u32[]{:S(2)}) collective-permute-start(bf16[192,320]{1,0:T(8,128)(2,1)S(1)} %get-tuple-element.119), channel_id=1, source_target_pairs={{0,1},{1,2},{4,5},{5,6},{8,9},{9,10},{12,13},{13,14},{16,17},{17,1... | collective-permute-start | bytes 368648 | tf_op jit(solution)/shard_map/ppermute | solution.py:865
  24.9 4.8 %collective-permute-start.5 = (bf16[192,320]{1,0:T(8,128)(2,1)S(1)}, bf16[192,320]{1,0:T(8,128)(2,1)S(1)}, u32[]{:S(2)}, u32[]{:S(2)}) collective-permute-start(bf16[192,320]{1,0:T(8,128)(2,1)S(1)} %get-tuple-element.128), channel_id=1, source_target_pairs={{1,2},{5,6},{9,10},{13,14},{17,18},{21,22},{25,26},{29,30},{33,34}... | collective-permute-start | bytes 368648 | tf_op jit(solution)/shard_map/ppermute | solution.py:865
  25.6 7.0 %collective-permute-start.4 = (bf16[192,320]{1,0:T(8,128)(2,1)S(1)}, bf16[192,320]{1,0:T(8,128)(2,1)S(1)}, u32[]{:S(2)}, u32[]{:S(2)}) collective-permute-start(bf16[192,320]{1,0:T(8,128)(2,1)S(1)} %get-tuple-element.112), channel_id=1, source_target_pairs={{0,3},{4,7},{8,11},{12,15},{16,19},{20,23},{24,27},{28,31},{32,35}... | collective-permute-start | bytes 368648 | tf_op jit(solution)/shard_map/ppermute | solution.py:867
  27.7 4.8 %collective-permute-start.3 = (bf16[192,320]{1,0:T(8,128)(2,1)S(1)}, bf16[192,320]{1,0:T(8,128)(2,1)S(1)}, u32[]{:S(2)}, u32[]{:S(2)}) collective-permute-start(bf16[192,320]{1,0:T(8,128)(2,1)S(1)} %get-tuple-element.127), channel_id=1, source_target_pairs={{1,2},{2,3},{5,6},{6,7},{9,10},{10,11},{13,14},{14,15},{17,18},{18... | collective-permute-start | bytes 368648 | tf_op jit(solution)/shard_map/ppermute | solution.py:865
  28.4 6.4 %collective-permute-start.10 = (bf16[192,320]{1,0:T(8,128)(2,1)S(1)}, bf16[192,320]{1,0:T(8,128)(2,1)S(1)}, u32[]{:S(2)}, u32[]{:S(2)}) collective-permute-start(bf16[192,320]{1,0:T(8,128)(2,1)S(1)} %get-tuple-element.120), channel_id=1, source_target_pairs={{0,3},{4,7},{8,11},{12,15},{16,19},{20,23},{24,27},{28,31},{32,35}... | collective-permute-start | bytes 368648 | tf_op jit(solution)/shard_map/ppermute | solution.py:867
  30.5 4.2 %collective-permute-start.9 = (bf16[192,320]{1,0:T(8,128)(2,1)S(1)}, bf16[192,320]{1,0:T(8,128)(2,1)S(1)}, u32[]{:S(2)}, u32[]{:S(2)}) collective-permute-start(bf16[192,320]{1,0:T(8,128)(2,1)S(1)} %get-tuple-element.136), channel_id=1, source_target_pairs={{2,3},{6,7},{10,11},{14,15},{18,19},{22,23},{26,27},{30,31},{34,35... | collective-permute-start | bytes 368648 | tf_op jit(solution)/shard_map/ppermute | solution.py:865
  31.2 5.1 %collective-permute-start.8 = (bf16[192,320]{1,0:T(8,128)(2,1)S(1)}, bf16[192,320]{1,0:T(8,128)(2,1)S(1)}, u32[]{:S(2)}, u32[]{:S(2)}) collective-permute-start(bf16[192,320]{1,0:T(8,128)(2,1)S(1)} %get-tuple-element.119), channel_id=1, source_target_pairs={{0,3},{4,7},{8,11},{12,15},{16,19},{20,23},{24,27},{28,31},{32,35}... | collective-permute-start | bytes 368648 | tf_op jit(solution)/shard_map/ppermute | solution.py:867
  33.4 2.9 %collective-permute-start.7 = (bf16[192,320]{1,0:T(8,128)(2,1)S(1)}, bf16[192,320]{1,0:T(8,128)(2,1)S(1)}, u32[]{:S(2)}, u32[]{:S(2)}) collective-permute-start(bf16[192,320]{1,0:T(8,128)(2,1)S(1)} %get-tuple-element.135), channel_id=1, source_target_pairs={{2,3},{6,7},{10,11},{14,15},{18,19},{22,23},{26,27},{30,31},{34,35... | collective-permute-start | bytes 368648 | tf_op jit(solution)/shard_map/ppermute | solution.py:865
  34.1 3.3 %collective-permute-start.6 = (bf16[192,320]{1,0:T(8,128)(2,1)S(1)}, bf16[192,320]{1,0:T(8,128)(2,1)S(1)}, u32[]{:S(2)}, u32[]{:S(2)}) collective-permute-start(bf16[192,320]{1,0:T(8,128)(2,1)S(1)} %get-tuple-element.135), channel_id=1, source_target_pairs={{3,2},{7,6},{11,10},{15,14},{19,18},{23,22},{27,26},{31,30},{35,34... | collective-permute-start | bytes 368648 | tf_op jit(solution)/shard_map/ppermute | solution.py:870
  35.6 5.2 %collective-permute-start.13 = (bf16[192,320]{1,0:T(8,128)(2,1)S(1)}, bf16[192,320]{1,0:T(8,128)(2,1)S(1)}, u32[]{:S(2)}, u32[]{:S(2)}) collective-permute-start(bf16[192,320]{1,0:T(8,128)(2,1)S(1)} %get-tuple-element.165), channel_id=1, source_target_pairs={{3,2},{7,6},{11,10},{15,14},{19,18},{23,22},{27,26},{31,30},{35,34... | collective-permute-start | bytes 368648 | tf_op jit(solution)/shard_map/ppermute | solution.py:870
  38.2 4.2 %collective-permute-start.11 = (bf16[192,320]{1,0:T(8,128)(2,1)S(1)}, bf16[192,320]{1,0:T(8,128)(2,1)S(1)}, u32[]{:S(2)}, u32[]{:S(2)}) collective-permute-start(bf16[192,320]{1,0:T(8,128)(2,1)S(1)} %get-tuple-element.163), channel_id=1, source_target_pairs={{2,1},{6,5},{10,9},{14,13},{18,17},{22,21},{26,25},{30,29},{34,33}... | collective-permute-start | bytes 368648 | tf_op jit(solution)/shard_map/ppermute | solution.py:898
  38.9 3.5 %collective-permute-start.12 = (bf16[192,320]{1,0:T(8,128)(2,1)S(1)}, bf16[192,320]{1,0:T(8,128)(2,1)S(1)}, u32[]{:S(2)}, u32[]{:S(2)}) collective-permute-start(bf16[192,320]{1,0:T(8,128)(2,1)S(1)} %get-tuple-element.164), channel_id=1, source_target_pairs={{3,2},{7,6},{11,10},{15,14},{19,18},{23,22},{27,26},{31,30},{35,34... | collective-permute-start | bytes 368648 | tf_op jit(solution)/shard_map/ppermute | solution.py:870
  39.6 33.5 %collective-permute-start.15 = (bf16[192,320]{1,0:T(8,128)(2,1)S(1)}, bf16[192,320]{1,0:T(8,128)(2,1)S(1)}, u32[]{:S(2)}, u32[]{:S(2)}) collective-permute-start(bf16[192,320]{1,0:T(8,128)(2,1)S(1)} %get-tuple-element.179), channel_id=1, source_target_pairs={{3,0},{7,4},{11,8},{15,12},{19,16},{23,20},{27,24},{31,28},{35,32}... | collective-permute-start | bytes 368648 | tf_op jit(solution)/shard_map/ppermute | solution.py:871
  41.7 5.4 %collective-permute-start.16 = (bf16[192,320]{1,0:T(8,128)(2,1)S(1)}, bf16[192,320]{1,0:T(8,128)(2,1)S(1)}, u32[]{:S(2)}, u32[]{:S(2)}) collective-permute-start(bf16[192,320]{1,0:T(8,128)(2,1)S(1)} %get-tuple-element.180), channel_id=1, source_target_pairs={{2,1},{6,5},{10,9},{14,13},{18,17},{22,21},{26,25},{30,29},{34,33}... | collective-permute-start | bytes 368648 | tf_op jit(solution)/shard_map/ppermute | solution.py:898
  43.3 34.9 %collective-permute-start.14 = (bf16[192,320]{1,0:T(8,128)(2,1)S(1)}, bf16[192,320]{1,0:T(8,128)(2,1)S(1)}, u32[]{:S(2)}, u32[]{:S(2)}) collective-permute-start(bf16[192,320]{1,0:T(8,128)(2,1)S(1)} %get-tuple-element.178), channel_id=1, source_target_pairs={{1,0},{2,1},{5,4},{6,5},{9,8},{10,9},{13,12},{14,13},{17,16},{18,1... | collective-permute-start | bytes 368648 | tf_op jit(solution)/shard_map/ppermute | solution.py:898
  44.6 42.2 %collective-permute-start.20 = (bf16[192,320]{1,0:T(8,128)(2,1)S(1)}, bf16[192,320]{1,0:T(8,128)(2,1)S(1)}, u32[]{:S(2)}, u32[]{:S(2)}) collective-permute-start(bf16[192,320]{1,0:T(8,128)(2,1)S(1)} %get-tuple-element.196), channel_id=1, source_target_pairs={{3,0},{7,4},{11,8},{15,12},{19,16},{23,20},{27,24},{31,28},{35,32}... | collective-permute-start | bytes 368648 | tf_op jit(solution)/shard_map/ppermute | solution.py:871
  45.9 48.1 %collective-permute-start.18 = (bf16[192,320]{1,0:T(8,128)(2,1)S(1)}, bf16[192,320]{1,0:T(8,128)(2,1)S(1)}, u32[]{:S(2)}, u32[]{:S(2)}) collective-permute-start(bf16[192,320]{1,0:T(8,128)(2,1)S(1)} %get-tuple-element.194), channel_id=1, source_target_pairs={{3,0},{7,4},{11,8},{15,12},{19,16},{23,20},{27,24},{31,28},{35,32}... | collective-permute-start | bytes 368648 | tf_op jit(solution)/shard_map/ppermute | solution.py:871
  48.0 39.3 %collective-permute-start.19 = (bf16[192,320]{1,0:T(8,128)(2,1)S(1)}, bf16[192,320]{1,0:T(8,128)(2,1)S(1)}, u32[]{:S(2)}, u32[]{:S(2)}) collective-permute-start(bf16[192,320]{1,0:T(8,128)(2,1)S(1)} %get-tuple-element.195), channel_id=1, source_target_pairs={{1,0},{5,4},{9,8},{13,12},{17,16},{21,20},{25,24},{29,28},{33,32},... | collective-permute-start | bytes 368648 | tf_op jit(solution)/shard_map/ppermute | solution.py:898
  84.9 10.2 %collective-permute-start.17 = (bf16[192,320]{1,0:T(8,128)(2,1)S(1)}, bf16[192,320]{1,0:T(8,128)(2,1)S(1)}, u32[]{:S(2)}, u32[]{:S(2)}) collective-permute-start(bf16[192,320]{1,0:T(8,128)(2,1)S(1)} %get-tuple-element.193), channel_id=1, source_target_pairs={{1,0},{5,4},{9,8},{13,12},{17,16},{21,20},{25,24},{29,28},{33,32},... | collective-permute-start | bytes 368648 | tf_op jit(solution)/shard_map/ppermute | solution.py:898
  101.8 0.6 copy-start.3
  110.0 8.8 %collective-permute-start.28 = (bf16[4,8,40,640]{3,2,1,0:T(8,128)(2,1)}, bf16[4,8,40,640]{3,2,1,0:T(8,128)(2,1)}, u32[]{:S(2)}, u32[]{:S(2)}) collective-permute-start(bf16[4,8,40,640]{3,2,1,0:T(8,128)(2,1)} %get-tuple-element.219), channel_id=1, source_target_pairs={{0,4},{4,0},{1,5},{5,1},{2,6},{6,2},{3,7},{7,3},{8,12},{12,8},{9,1... | collective-permute-start | bytes 4915208 | tf_op jit(solution)/shard_map/ppermute | solution.py:921
  118.2 7.2 %collective-permute-start.21 = (bf16[4,8,40,640]{3,2,1,0:T(8,128)(2,1)}, bf16[4,8,40,640]{3,2,1,0:T(8,128)(2,1)S(1)}, u32[]{:S(2)}, u32[]{:S(2)}) collective-permute-start(bf16[4,8,40,640]{3,2,1,0:T(8,128)(2,1)} %get-tuple-element.213), channel_id=1, source_target_pairs={{0,4},{4,0},{1,5},{5,1},{2,6},{6,2},{3,7},{7,3},{8,12},{12,8},{9,1... | collective-permute-start | bytes 4915208 | tf_op jit(solution)/shard_map/ppermute | solution.py:910
  121.1 4.4 %copy-start.5 = (bf16[4,8,40,640]{3,2,1,0:T(8,128)(2,1)S(1)}, bf16[4,8,40,640]{3,2,1,0:T(8,128)(2,1)}, u32[]{:S(2)}) copy-start(bf16[4,8,40,640]{3,2,1,0:T(8,128)(2,1)} %get-tuple-element.212) | copy-start | bytes 4915204
  121.2 13.0 %collective-permute-start.29 = (bf16[8,40,640]{2,1,0:T(8,128)(2,1)S(1)}, bf16[8,40,640]{2,1,0:T(8,128)(2,1)S(1)}, u32[]{:S(2)}, u32[]{:S(2)}) collective-permute-start(bf16[8,40,640]{2,1,0:T(8,128)(2,1)S(1)} %pad_maximum_fusion.4), channel_id=1, source_target_pairs={{0,96},{32,0},{64,32},{96,64},{1,97},{33,1},{65,33},{97,65},{2,98}... | collective-permute-start | bytes 1228808 | tf_op jit(solution)/shard_map/ppermute | solution.py:806
  125.4 12.7 %collective-permute-start.30 = (bf16[8,40,640]{2,1,0:T(8,128)(2,1)S(1)}, bf16[8,40,640]{2,1,0:T(8,128)(2,1)S(1)}, u32[]{:S(2)}, u32[]{:S(2)}) collective-permute-start(bf16[8,40,640]{2,1,0:T(8,128)(2,1)S(1)} %pad_maximum_fusion.5), channel_id=1, source_target_pairs={{0,32},{32,64},{64,96},{96,0},{1,33},{33,65},{65,97},{97,1},{2,34}... | collective-permute-start | bytes 1228808 | tf_op jit(solution)/shard_map/ppermute | solution.py:805
  126.0 12.2 %collective-permute-start.22 = (bf16[8,40,640]{2,1,0:T(8,128)(2,1)S(1)}, bf16[8,40,640]{2,1,0:T(8,128)(2,1)S(1)}, u32[]{:S(2)}, u32[]{:S(2)}) collective-permute-start(bf16[8,40,640]{2,1,0:T(8,128)(2,1)S(1)} %pad_maximum_fusion.1), channel_id=1, source_target_pairs={{0,24},{8,0},{16,8},{24,16},{1,25},{9,1},{17,9},{25,17},{2,26},{10... | collective-permute-start | bytes 1228808 | tf_op jit(solution)/shard_map/ppermute | solution.py:806
  129.0 13.1 %collective-permute-start.23 = (bf16[8,40,640]{2,1,0:T(8,128)(2,1)S(1)}, bf16[8,40,640]{2,1,0:T(8,128)(2,1)S(1)}, u32[]{:S(2)}, u32[]{:S(2)}) collective-permute-start(bf16[8,40,640]{2,1,0:T(8,128)(2,1)S(1)} %pad_maximum_fusion.2), channel_id=1, source_target_pairs={{0,8},{8,16},{16,24},{24,0},{1,9},{9,17},{17,25},{25,1},{2,10},{10... | collective-permute-start | bytes 1228808 | tf_op jit(solution)/shard_map/ppermute | solution.py:805
  134.3 8.5 %collective-permute-start.32 = (bf16[4,40,640]{2,1,0:T(8,128)(2,1)S(1)}, bf16[4,40,640]{2,1,0:T(8,128)(2,1)S(1)}, u32[]{:S(2)}, u32[]{:S(2)}) collective-permute-start(bf16[4,40,640]{2,1,0:T(8,128)(2,1)S(1)} %fusion.2), channel_id=1, source_target_pairs={{0,96},{32,0},{64,32},{96,64},{1,97},{33,1},{65,33},{97,65},{2,98}... | collective-permute-start | bytes 614408 | tf_op jit(solution)/shard_map/ppermute | solution.py:809
  138.2 7.2 %collective-permute-start.31 = (bf16[4,40,640]{2,1,0:T(8,128)(2,1)S(1)}, bf16[4,40,640]{2,1,0:T(8,128)(2,1)S(1)}, u32[]{:S(2)}, u32[]{:S(2)}) collective-permute-start(bf16[4,40,640]{2,1,0:T(8,128)(2,1)S(1)} %fusion.5), channel_id=1, source_target_pairs={{0,32},{32,64},{64,96},{96,0},{1,33},{33,65},{65,97},{97,1},{2,34}... | collective-permute-start | bytes 614408 | tf_op jit(solution)/shard_map/ppermute | solution.py:808
  139.0 9.0 %collective-permute-start.25 = (bf16[4,40,640]{2,1,0:T(8,128)(2,1)}, bf16[4,40,640]{2,1,0:T(8,128)(2,1)S(1)}, u32[]{:S(2)}, u32[]{:S(2)}) collective-permute-start(bf16[4,40,640]{2,1,0:T(8,128)(2,1)} %fusion.8), channel_id=1, source_target_pairs={{0,24},{8,0},{16,8},{24,16},{1,25},{9,1},{17,9},{25,17},{2,26},{10... | collective-permute-start | bytes 614408 | tf_op jit(solution)/shard_map/ppermute | solution.py:809
  142.0 3.4 %copy-start.6 = (bf16[8,40,640]{2,1,0:T(8,128)(2,1)}, bf16[8,40,640]{2,1,0:T(8,128)(2,1)S(1)}, u32[]{:S(2)}) copy-start(bf16[8,40,640]{2,1,0:T(8,128)(2,1)S(1)} %collective-permute-done.23) | copy-start | bytes 1228804
  142.8 7.3 %collective-permute-start.24 = (bf16[4,40,640]{2,1,0:T(8,128)(2,1)}, bf16[4,40,640]{2,1,0:T(8,128)(2,1)}, u32[]{:S(2)}, u32[]{:S(2)}) collective-permute-start(bf16[4,40,640]{2,1,0:T(8,128)(2,1)} %fusion.11), channel_id=1, source_target_pairs={{0,8},{8,16},{16,24},{24,0},{1,9},{9,17},{17,25},{25,1},{2,10},{10... | collective-permute-start | bytes 614408 | tf_op jit(solution)/shard_map/ppermute | solution.py:808
  146.4 6.1 %collective-permute-start.33 = (bf16[2,150,320]{2,1,0:T(8,128)(2,1)S(1)}, bf16[2,150,320]{2,1,0:T(8,128)(2,1)S(1)}, u32[]{:S(2)}, u32[]{:S(2)}) collective-permute-start(bf16[2,150,320]{2,1,0:T(8,128)(2,1)S(1)} %pad_maximum_fusion.7), channel_id=1, source_target_pairs={{0,8},{8,0},{16,24},{24,16},{1,9},{9,1},{17,25},{25,17},{2,10},{10... | collective-permute-start | bytes 576008 | tf_op jit(solution)/shard_map/ppermute | solution.py:793
  151.5 5.8 %collective-permute-start.26 = (bf16[2,8,10,640]{3,1,2,0:T(8,128)(2,1)S(1)}, bf16[2,8,10,640]{3,1,2,0:T(8,128)(2,1)S(1)}, u32[]{:S(2)}, u32[]{:S(2)}) collective-permute-start(bf16[2,8,10,640]{3,1,2,0:T(8,128)(2,1)S(1)} %pad_maximum_fusion.8), channel_id=1, source_target_pairs={{0,32},{32,0},{64,96},{96,64},{1,33},{33,1},{65,97},{97,65},{2,34}... | collective-permute-start | bytes 614408 | tf_op jit(solution)/shard_map/ppermute | solution.py:793
  152.6 7.8 %collective-permute-start.34 = (bf16[150,320]{1,0:T(8,128)(2,1)S(1)}, bf16[150,320]{1,0:T(8,128)(2,1)S(1)}, u32[]{:S(2)}, u32[]{:S(2)}) collective-permute-start(bf16[150,320]{1,0:T(8,128)(2,1)S(1)} %fusion.16), channel_id=1, source_target_pairs={{0,24},{8,16},{16,8},{24,0},{1,25},{9,17},{17,9},{25,1},{2,26},{10... | collective-permute-start | bytes 288008 | tf_op jit(solution)/shard_map/ppermute | solution.py:795
  157.4 6.0 %collective-permute-start.27 = (bf16[8,10,640]{2,0,1:T(8,128)(2,1)S(1)}, bf16[8,10,640]{2,0,1:T(8,128)(2,1)S(1)}, u32[]{:S(2)}, u32[]{:S(2)}) collective-permute-start(bf16[8,10,640]{2,0,1:T(8,128)(2,1)S(1)} %fusion.14), channel_id=1, source_target_pairs={{0,96},{32,64},{64,32},{96,0},{1,97},{33,65},{65,33},{97,1},{2,98}... | collective-permute-start | bytes 307208 | tf_op jit(solution)/shard_map/ppermute | solution.py:795
